TPU v7x, 512 devices: a whole 4x8x8 slice. The times are simulated.
512 devices in a mesh: gx: 8 (over z), gy: 8 (over y), gz: 8 (over x, core).
Axes of the slice: x: 4, y: 8, z: 8, core: 2. Of those that a mesh axis runs over, the one named last changes fastest.
Arguments:
- electric: float32 [3, 64, 128, 1024], P(None, 'gx', 'gy', 'gz'), may hold values from -6 to 6
- electric_prev: float32 [3, 64, 128, 1024], P(None, 'gx', 'gy', 'gz'), may hold values from -6 to 6
- courant: float32 [64, 128, 1024], P('gx', 'gy', 'gz'), may hold values from 0.05 to 0.25
- port_cell: int32 [131072], P(('gx', 'gy', 'gz')), may hold values from 0 to 16383
- port_route: int32 [131072, 1], P(('gx', 'gy', 'gz')), may hold values from 0 to 63; in each aligned block of 256 rows (0 to 255, 256 to 511, ...) at most 8 rows name the same one
- port_group: int32 [131072], P(('gx', 'gy', 'gz')), may hold values from 0 to 7
- port_gain: float32 [131072], P(('gx', 'gy', 'gz')), may hold values from 0.5 to 2
- port_drive: float32 [131072], P(('gx', 'gy', 'gz')), may hold values from 0.3 to 3
- port_bias: float32 [131072], P(('gx', 'gy', 'gz')), may hold values from -5 to 5
- port_couple: float32 [131072], P(('gx', 'gy', 'gz')), may hold values from 0.02 to 0.08
Outputs:
- electric_next: float32 [3, 64, 128, 1024], P(None, 'gx', 'gy', 'gz')
- electric_last: float32 [3, 64, 128, 1024], P(None, 'gx', 'gy', 'gz')
- port_current: float32 [131072], P(('gx', 'gy', 'gz'))
Inputs may be any that keep to these rules, and one draw needn't show every extreme that they name: Of the ports of one device, at most 8 have the same port_route, and in every draw some device has exactly 8 ports of one port_route.
All inputs are finite; a program needn't handle non-finite values.
Results may differ from a plain program's by a relative error of at most 0.00015.
Values sent between devices are 32-bit elements; how exact they have to be, the bound alone decides.
A program may use at most 64 MiB of HBM per device.

v0:
```python
import jax
import jax.numpy as jnp
from jax import lax
from jax.sharding import PartitionSpec as P

SUB = 4
ITERS = 3
GROUPS = 8


def with_halo(block, sides, width):
    for axis, dim in sides:
        count = lax.axis_size(axis)
        forward = [(i, i + 1) for i in range(count - 1)]
        backward = [(target, source) for source, target in forward]
        low = lax.ppermute(
            lax.slice_in_dim(block, block.shape[dim] - width, None, axis=dim), axis, forward
        )
        high = lax.ppermute(lax.slice_in_dim(block, 0, width, axis=dim), axis, backward)
        block = jnp.concatenate([low, block, high], axis=dim)
    return block


def curl_curl(padded):
    field_x, field_y, field_z = (padded[0], padded[1], padded[2])
    curl_x = (
        field_z[:-1, 1:, :-1]
        - field_z[:-1, :-1, :-1]
        - (field_y[:-1, :-1, 1:] - field_y[:-1, :-1, :-1])
    )
    curl_y = (
        field_x[:-1, :-1, 1:]
        - field_x[:-1, :-1, :-1]
        - (field_z[1:, :-1, :-1] - field_z[:-1, :-1, :-1])
    )
    curl_z = (
        field_y[1:, :-1, :-1]
        - field_y[:-1, :-1, :-1]
        - (field_x[:-1, 1:, :-1] - field_x[:-1, :-1, :-1])
    )
    back_x = curl_z[1:, 1:, 1:] - curl_z[1:, :-1, 1:] - (curl_y[1:, 1:, 1:] - curl_y[1:, 1:, :-1])
    back_y = curl_x[1:, 1:, 1:] - curl_x[1:, 1:, :-1] - (curl_z[1:, 1:, 1:] - curl_z[:-1, 1:, 1:])
    back_z = curl_y[1:, 1:, 1:] - curl_y[:-1, 1:, 1:] - (curl_x[1:, 1:, 1:] - curl_x[1:, :-1, 1:])
    return jnp.stack([back_x, back_y, back_z])


def solve_drivers(incoming):
    volt_in, gain_in, drive_in = (incoming[0], incoming[1], incoming[2])
    bias_in, couple_in, group_in, valid_in = (incoming[3], incoming[4], incoming[5], incoming[6])
    member = (group_in[None, :] == jnp.arange(GROUPS, dtype=jnp.float32)[:, None]).astype(
        jnp.float32
    )
    node_volt = volt_in
    for iterate in range(ITERS):
        squash = jnp.tanh(node_volt)
        totals = jnp.dot(member, valid_in * squash, precision=lax.Precision.HIGHEST)
        shared = jnp.dot(totals, member, precision=lax.Precision.HIGHEST)
        resid = (
            (1.0 + gain_in) * node_volt - volt_in - bias_in + drive_in * squash + couple_in * shared
        )
        slope_diag = 1.0 + gain_in + (drive_in + couple_in) * (1.0 - squash * squash)
        node_volt = node_volt - resid / slope_diag
    return gain_in * (node_volt - volt_in)


def on_device(
    electric,
    electric_prev,
    courant,
    port_cell,
    port_route,
    port_group,
    port_gain,
    port_drive,
    port_bias,
    port_couple,
):
    size_x, size_y, size_z = (electric.shape[1], electric.shape[2], electric.shape[3])
    present, previous = (electric, electric_prev)
    for substep in range(SUB):
        padded = with_halo(present, (("gx", 1), ("gy", 2), ("gz", 3)), 1)
        updated = 2.0 * present - previous - courant[None] * curl_curl(padded)
        previous, present = (present, updated)
    ez_flat = present[2].reshape(-1)
    sample = ez_flat[port_cell]
    side_y = lax.axis_size("gy")
    side_z = lax.axis_size("gz")
    peer_count = side_y * side_z
    ports_here = port_cell.shape[0]
    route_dest = port_route[:, 0]
    capacity = max(2, 2 * ports_here // peer_count)
    onehot = (route_dest[:, None] == jnp.arange(peer_count, dtype=jnp.int32)[None, :]).astype(
        jnp.int32
    )
    rank_slot = jnp.sum(jnp.cumsum(onehot, axis=0) * onehot, axis=1) - 1
    target = route_dest * capacity + rank_slot
    payload = jnp.stack(
        [
            sample,
            port_gain,
            port_drive,
            port_bias,
            port_couple,
            port_group.astype(jnp.float32),
            jnp.ones_like(sample),
        ]
    )
    outgoing = jnp.zeros((7, peer_count * capacity), jnp.float32).at[:, target].set(payload)
    incoming = lax.all_to_all(outgoing, ("gy", "gz"), split_axis=1, concat_axis=1, tiled=True)
    answer = solve_drivers(incoming)
    returned = lax.all_to_all(answer[None], ("gy", "gz"), split_axis=1, concat_axis=1, tiled=True)[
        0
    ]
    current = returned[target]
    ez_next = ez_flat.at[port_cell].add(current).reshape(size_x, size_y, size_z)
    return (present.at[2].set(ez_next), previous, current)


def solution(mesh):
    placed = (
        P(None, "gx", "gy", "gz"),
        P(None, "gx", "gy", "gz"),
        P("gx", "gy", "gz"),
        P(("gx", "gy", "gz")),
        P(("gx", "gy", "gz"), None),
        P(("gx", "gy", "gz")),
        P(("gx", "gy", "gz")),
        P(("gx", "gy", "gz")),
        P(("gx", "gy", "gz")),
        P(("gx", "gy", "gz")),
    )
    return jax.shard_map(
        on_device,
        mesh=mesh,
        in_specs=placed,
        out_specs=(P(None, "gx", "gy", "gz"), P(None, "gx", "gy", "gz"), P(("gx", "gy", "gz"))),
        check_vma=False,
    )
```

profile of v0, /device:TPU:1, one launch (start us, length us, event | category | flops | bytes accessed | tf_op | source)
XLA Modules:
  0.0 180.7 jit_solution(4567110113378674815)
XLA Ops:
  1.4 4.8 %collective-permute-start = (f32[3,1,16,128]{3,2,1,0:T(8,128)S(1)}, f32[3,1,16,128]{3,2,1,0:T(8,128)S(1)}, u32[]{:S(2)}, u32[]{:S(2)}) collective-permute-start(f32[3,1,16,128]{3,2,1,0:T(8,128)S(1)} %get-tuple-element.86), channel_id=1, source_target_pairs={{0,64},{64,128},{128,192},{192,256},{256,320},{320,384},{384,448},... | collective-permute-start | bytes 73736 | tf_op jit(solution)/shard_map/ppermute | solution.py:16
  8.5 2.9 %collective-permute-done.1 = f32[3,1,16,128]{3,2,1,0:T(8,128)S(1)} collective-permute-done((f32[3,1,16,128]{3,2,1,0:T(8,128)S(1)}, f32[3,1,16,128]{3,2,1,0:T(8,128)S(1)}, u32[]{:S(2)}, u32[]{:S(2)}) %collective-permute-start.1) | collective-permute-done | bytes 24608 | tf_op jit(solution)/shard_map/ppermute | solution.py:19
  11.5 3.2 %collective-permute-start.2 = (f32[3,10,1,128]{3,2,1,0:T(1,128)S(1)}, f32[3,10,1,128]{3,2,1,0:T(1,128)S(1)}, u32[]{:S(2)}, u32[]{:S(2)}) collective-permute-start(f32[3,10,1,128]{3,2,1,0:T(1,128)S(1)} %get-tuple-element.65), channel_id=1, source_target_pairs={{0,8},{8,16},{16,24},{24,32},{32,40},{40,48},{48,56},{1,9},{9,17},... | collective-permute-start | bytes 46088 | tf_op jit(solution)/shard_map/ppermute | solution.py:16
  16.0 3.2 %collective-permute-done.3 = f32[3,10,1,128]{3,2,1,0:T(1,128)S(1)} collective-permute-done((f32[3,10,1,128]{3,2,1,0:T(1,128)S(1)}, f32[3,10,1,128]{3,2,1,0:T(1,128)S(1)}, u32[]{:S(2)}, u32[]{:S(2)}) %collective-permute-start.3) | collective-permute-done | bytes 15392 | tf_op jit(solution)/shard_map/ppermute | solution.py:19
  19.4 6.3 %collective-permute-start.4 = (f32[3,10,18,1]{3,2,1,0:T(8,128)S(1)}, f32[3,10,18,1]{3,2,1,0:T(8,128)S(1)}, u32[]{:S(2)}, u32[]{:S(2)}) collective-permute-start(f32[3,10,18,1]{3,2,1,0:T(8,128)S(1)} %get-tuple-element.45), channel_id=1, source_target_pairs={{0,1},{1,2},{2,3},{3,4},{4,5},{5,6},{6,7},{8,9},{9,10},{10,11},{11... | collective-permute-start | bytes 6488 | tf_op jit(solution)/shard_map/ppermute | solution.py:16
  27.6 2.5 %collective-permute-done.4 = f32[3,10,18,1]{3,2,1,0:T(8,128)S(1)} collective-permute-done((f32[3,10,18,1]{3,2,1,0:T(8,128)S(1)}, f32[3,10,18,1]{3,2,1,0:T(8,128)S(1)}, u32[]{:S(2)}, u32[]{:S(2)}) %collective-permute-start.4) | collective-permute-done | bytes 2192 | tf_op jit(solution)/shard_map/ppermute | solution.py:16
  30.1 4.4 %collective-permute-done.5 = f32[3,10,18,1]{3,2,1,0:T(8,128)S(1)} collective-permute-done((f32[3,10,18,1]{3,2,1,0:T(8,128)S(1)}, f32[3,10,18,1]{3,2,1,0:T(8,128)S(1)}, u32[]{:S(2)}, u32[]{:S(2)}) %collective-permute-start.5) | collective-permute-done | bytes 2192 | tf_op jit(solution)/shard_map/ppermute | solution.py:19
  36.3 4.0 %collective-permute-start.6 = (f32[3,1,16,128]{3,2,1,0:T(8,128)S(1)}, f32[3,1,16,128]{3,2,1,0:T(8,128)S(1)}, u32[]{:S(2)}, u32[]{:S(2)}) collective-permute-start(f32[3,1,16,128]{3,2,1,0:T(8,128)S(1)} %get-tuple-element.83), channel_id=1, source_target_pairs={{0,64},{64,128},{128,192},{192,256},{256,320},{320,384},{384,448},... | collective-permute-start | bytes 73736 | tf_op jit(solution)/shard_map/ppermute | solution.py:16
  41.7 5.1 %collective-permute-done.7 = f32[3,1,16,128]{3,2,1,0:T(8,128)S(1)} collective-permute-done((f32[3,1,16,128]{3,2,1,0:T(8,128)S(1)}, f32[3,1,16,128]{3,2,1,0:T(8,128)S(1)}, u32[]{:S(2)}, u32[]{:S(2)}) %collective-permute-start.7) | collective-permute-done | bytes 24608 | tf_op jit(solution)/shard_map/ppermute | solution.py:19
  46.8 3.2 %collective-permute-start.8 = (f32[3,10,1,128]{3,2,1,0:T(1,128)S(1)}, f32[3,10,1,128]{3,2,1,0:T(1,128)S(1)}, u32[]{:S(2)}, u32[]{:S(2)}) collective-permute-start(f32[3,10,1,128]{3,2,1,0:T(1,128)S(1)} %get-tuple-element.60), channel_id=1, source_target_pairs={{0,8},{8,16},{16,24},{24,32},{32,40},{40,48},{48,56},{1,9},{9,17},... | collective-permute-start | bytes 46088 | tf_op jit(solution)/shard_map/ppermute | solution.py:16
  51.3 3.8 %collective-permute-done.9 = f32[3,10,1,128]{3,2,1,0:T(1,128)S(1)} collective-permute-done((f32[3,10,1,128]{3,2,1,0:T(1,128)S(1)}, f32[3,10,1,128]{3,2,1,0:T(1,128)S(1)}, u32[]{:S(2)}, u32[]{:S(2)}) %collective-permute-start.9) | collective-permute-done | bytes 15392 | tf_op jit(solution)/shard_map/ppermute | solution.py:19
  55.3 4.0 %collective-permute-start.10 = (f32[3,10,18,1]{3,2,1,0:T(8,128)S(1)}, f32[3,10,18,1]{3,2,1,0:T(8,128)S(1)}, u32[]{:S(2)}, u32[]{:S(2)}) collective-permute-start(f32[3,10,18,1]{3,2,1,0:T(8,128)S(1)} %get-tuple-element.43), channel_id=1, source_target_pairs={{0,1},{1,2},{2,3},{3,4},{4,5},{5,6},{6,7},{8,9},{9,10},{10,11},{11... | collective-permute-start | bytes 6488 | tf_op jit(solution)/shard_map/ppermute | solution.py:16
  63.8 4.4 %collective-permute-done.11 = f32[3,10,18,1]{3,2,1,0:T(8,128)S(1)} collective-permute-done((f32[3,10,18,1]{3,2,1,0:T(8,128)S(1)}, f32[3,10,18,1]{3,2,1,0:T(8,128)S(1)}, u32[]{:S(2)}, u32[]{:S(2)}) %collective-permute-start.11) | collective-permute-done | bytes 2192 | tf_op jit(solution)/shard_map/ppermute | solution.py:19
  69.2 4.8 %collective-permute-start.12 = (f32[3,1,16,128]{3,2,1,0:T(8,128)S(1)}, f32[3,1,16,128]{3,2,1,0:T(8,128)S(1)}, u32[]{:S(2)}, u32[]{:S(2)}) collective-permute-start(f32[3,1,16,128]{3,2,1,0:T(8,128)S(1)} %get-tuple-element.81), channel_id=1, source_target_pairs={{0,64},{64,128},{128,192},{192,256},{256,320},{320,384},{384,448},... | collective-permute-start | bytes 73736 | tf_op jit(solution)/shard_map/ppermute | solution.py:16
  76.2 2.7 %collective-permute-done.13 = f32[3,1,16,128]{3,2,1,0:T(8,128)S(1)} collective-permute-done((f32[3,1,16,128]{3,2,1,0:T(8,128)S(1)}, f32[3,1,16,128]{3,2,1,0:T(8,128)S(1)}, u32[]{:S(2)}, u32[]{:S(2)}) %collective-permute-start.13) | collective-permute-done | bytes 24608 | tf_op jit(solution)/shard_map/ppermute | solution.py:19
  79.0 4.8 %collective-permute-start.14 = (f32[3,10,1,128]{3,2,1,0:T(1,128)S(1)}, f32[3,10,1,128]{3,2,1,0:T(1,128)S(1)}, u32[]{:S(2)}, u32[]{:S(2)}) collective-permute-start(f32[3,10,1,128]{3,2,1,0:T(1,128)S(1)} %get-tuple-element.55), channel_id=1, source_target_pairs={{0,8},{8,16},{16,24},{24,32},{32,40},{40,48},{48,56},{1,9},{9,17},... | collective-permute-start | bytes 46088 | tf_op jit(solution)/shard_map/ppermute | solution.py:16
  85.3 3.3 %collective-permute-done.15 = f32[3,10,1,128]{3,2,1,0:T(1,128)S(1)} collective-permute-done((f32[3,10,1,128]{3,2,1,0:T(1,128)S(1)}, f32[3,10,1,128]{3,2,1,0:T(1,128)S(1)}, u32[]{:S(2)}, u32[]{:S(2)}) %collective-permute-start.15) | collective-permute-done | bytes 15392 | tf_op jit(solution)/shard_map/ppermute | solution.py:19
  88.8 4.1 %collective-permute-start.16 = (f32[3,10,18,1]{3,2,1,0:T(8,128)S(1)}, f32[3,10,18,1]{3,2,1,0:T(8,128)S(1)}, u32[]{:S(2)}, u32[]{:S(2)}) collective-permute-start(f32[3,10,18,1]{3,2,1,0:T(8,128)S(1)} %get-tuple-element.41), channel_id=1, source_target_pairs={{0,1},{1,2},{2,3},{3,4},{4,5},{5,6},{6,7},{8,9},{9,10},{10,11},{11... | collective-permute-start | bytes 6488 | tf_op jit(solution)/shard_map/ppermute | solution.py:16
  94.8 2.5 %collective-permute-done.16 = f32[3,10,18,1]{3,2,1,0:T(8,128)S(1)} collective-permute-done((f32[3,10,18,1]{3,2,1,0:T(8,128)S(1)}, f32[3,10,18,1]{3,2,1,0:T(8,128)S(1)}, u32[]{:S(2)}, u32[]{:S(2)}) %collective-permute-start.16) | collective-permute-done | bytes 2192 | tf_op jit(solution)/shard_map/ppermute | solution.py:16
  97.3 4.4 %collective-permute-done.17 = f32[3,10,18,1]{3,2,1,0:T(8,128)S(1)} collective-permute-done((f32[3,10,18,1]{3,2,1,0:T(8,128)S(1)}, f32[3,10,18,1]{3,2,1,0:T(8,128)S(1)}, u32[]{:S(2)}, u32[]{:S(2)}) %collective-permute-start.17) | collective-permute-done | bytes 2192 | tf_op jit(solution)/shard_map/ppermute | solution.py:19
  102.7 3.6 %collective-permute-start.18 = (f32[3,1,16,128]{3,2,1,0:T(8,128)S(1)}, f32[3,1,16,128]{3,2,1,0:T(8,128)S(1)}, u32[]{:S(2)}, u32[]{:S(2)}) collective-permute-start(f32[3,1,16,128]{3,2,1,0:T(8,128)S(1)} %get-tuple-element.79), channel_id=1, source_target_pairs={{0,64},{64,128},{128,192},{192,256},{256,320},{320,384},{384,448},... | collective-permute-start | bytes 73736 | tf_op jit(solution)/shard_map/ppermute | solution.py:16
  107.7 3.2 %collective-permute-done.19 = f32[3,1,16,128]{3,2,1,0:T(8,128)S(1)} collective-permute-done((f32[3,1,16,128]{3,2,1,0:T(8,128)S(1)}, f32[3,1,16,128]{3,2,1,0:T(8,128)S(1)}, u32[]{:S(2)}, u32[]{:S(2)}) %collective-permute-start.19) | collective-permute-done | bytes 24608 | tf_op jit(solution)/shard_map/ppermute | solution.py:19
  111.0 3.6 %collective-permute-start.20 = (f32[3,10,1,128]{3,2,1,0:T(1,128)S(1)}, f32[3,10,1,128]{3,2,1,0:T(1,128)S(1)}, u32[]{:S(2)}, u32[]{:S(2)}) collective-permute-start(f32[3,10,1,128]{3,2,1,0:T(1,128)S(1)} %get-tuple-element.50), channel_id=1, source_target_pairs={{0,8},{8,16},{16,24},{24,32},{32,40},{40,48},{48,56},{1,9},{9,17},... | collective-permute-start | bytes 46088 | tf_op jit(solution)/shard_map/ppermute | solution.py:16
  116.0 3.1 %collective-permute-done.21 = f32[3,10,1,128]{3,2,1,0:T(1,128)S(1)} collective-permute-done((f32[3,10,1,128]{3,2,1,0:T(1,128)S(1)}, f32[3,10,1,128]{3,2,1,0:T(1,128)S(1)}, u32[]{:S(2)}, u32[]{:S(2)}) %collective-permute-start.21) | collective-permute-done | bytes 15392 | tf_op jit(solution)/shard_map/ppermute | solution.py:19
  119.4 4.6 %collective-permute-start.22 = (f32[3,10,18,1]{3,2,1,0:T(8,128)S(1)}, f32[3,10,18,1]{3,2,1,0:T(8,128)S(1)}, u32[]{:S(2)}, u32[]{:S(2)}) collective-permute-start(f32[3,10,18,1]{3,2,1,0:T(8,128)S(1)} %get-tuple-element.39), channel_id=1, source_target_pairs={{0,1},{1,2},{2,3},{3,4},{4,5},{5,6},{6,7},{8,9},{9,10},{10,11},{11... | collective-permute-start | bytes 6488 | tf_op jit(solution)/shard_map/ppermute | solution.py:16
  126.0 2.5 %collective-permute-done.22 = f32[3,10,18,1]{3,2,1,0:T(8,128)S(1)} collective-permute-done((f32[3,10,18,1]{3,2,1,0:T(8,128)S(1)}, f32[3,10,18,1]{3,2,1,0:T(8,128)S(1)}, u32[]{:S(2)}, u32[]{:S(2)}) %collective-permute-start.22) | collective-permute-done | bytes 2192 | tf_op jit(solution)/shard_map/ppermute | solution.py:16
  128.4 4.4 %collective-permute-done.23 = f32[3,10,18,1]{3,2,1,0:T(8,128)S(1)} collective-permute-done((f32[3,10,18,1]{3,2,1,0:T(8,128)S(1)}, f32[3,10,18,1]{3,2,1,0:T(8,128)S(1)}, u32[]{:S(2)}, u32[]{:S(2)}) %collective-permute-start.23) | collective-permute-done | bytes 2192 | tf_op jit(solution)/shard_map/ppermute | solution.py:19
  138.1 19.6 %all_to_all.18 = f32[7,64,8]{2,0,1:T(8,128)S(1)} all-to-all(f32[7,64,8]{2,0,1:T(8,128)S(1)} %copy.18), channel_id=1, replica_groups=mesh['gx'=8,'gy'=8,'gz'=8] {'gy','gz'}, dimensions={1} | all-to-all | bytes 28672 | tf_op jit(solution)/shard_map/all_to_all | solution.py:109
  160.7 4.7 %all-to-all-start.1 = ((f32[1,64,8]{2,0,1:T(1,128)}), f32[1,64,8]{2,0,1:T(1,128)S(1)}, u32[]{:S(2)}, u32[]{:S(2)}) async-start(f32[1,64,8]{2,0,1:T(1,128)} %bitcast.50), calls=%async_computation.1 | async-start | bytes 65536 | tf_op jit(solution)/shard_map/all_to_all | solution.py:111
  165.4 9.3 %all-to-all-done.1 = f32[1,64,8]{2,0,1:T(1,128)S(1)} async-done(((f32[1,64,8]{2,0,1:T(1,128)}), f32[1,64,8]{2,0,1:T(1,128)S(1)}, u32[]{:S(2)}, u32[]{:S(2)}) %all-to-all-start.1) | async-done | bytes 2080 | tf_op jit(solution)/shard_map/all_to_all | solution.py:111
  176.0 1.9 %gather_fusion.1 = f32[256]{0:T(256)S(1)} fusion(f32[512]{0:T(512)S(1)} %squeeze.76, s32[1024]{0:T(1024)S(1)} %pad_clamp_fusion), kind=kCustom, calls=%fused_computation.1 | custom fusion | bytes 3072 | tf_op jit(solution)/shard_map/gather | solution.py:114
  178.0 2.0 %scatter_fusion = f32[16384]{0:T(1024)S(1)} fusion(f32[16384]{0:T(1024)S(1)} %bitcast.101, s32[256]{0:T(256)S(1)} %compare_select_fusion.1, f32[256]{0:T(256)S(1)} %gather_fusion.1), kind=kCustom, calls=%fused_computation.3 | custom fusion | flops 256 | bytes 4096 | tf_op jit(solution)/shard_map/scatter-add | solution.py:115
  (131 shorter events, 38.0 us)
Async XLA Ops:
  1.4 6.1 %collective-permute-start = (f32[3,1,16,128]{3,2,1,0:T(8,128)S(1)}, f32[3,1,16,128]{3,2,1,0:T(8,128)S(1)}, u32[]{:S(2)}, u32[]{:S(2)}) collective-permute-start(f32[3,1,16,128]{3,2,1,0:T(8,128)S(1)} %get-tuple-element.86), channel_id=1, source_target_pairs={{0,64},{64,128},{128,192},{192,256},{256,320},{320,384},{384,448},... | collective-permute-start | bytes 73736 | tf_op jit(solution)/shard_map/ppermute | solution.py:16
  6.2 5.2 %collective-permute-start.1 = (f32[3,1,16,128]{3,2,1,0:T(8,128)S(1)}, f32[3,1,16,128]{3,2,1,0:T(8,128)S(1)}, u32[]{:S(2)}, u32[]{:S(2)}) collective-permute-start(f32[3,1,16,128]{3,2,1,0:T(8,128)S(1)} %get-tuple-element.85), channel_id=1, source_target_pairs={{64,0},{128,64},{192,128},{256,192},{320,256},{384,320},{448,384},... | collective-permute-start | bytes 73736 | tf_op jit(solution)/shard_map/ppermute | solution.py:19
  11.5 4.5 %collective-permute-start.2 = (f32[3,10,1,128]{3,2,1,0:T(1,128)S(1)}, f32[3,10,1,128]{3,2,1,0:T(1,128)S(1)}, u32[]{:S(2)}, u32[]{:S(2)}) collective-permute-start(f32[3,10,1,128]{3,2,1,0:T(1,128)S(1)} %get-tuple-element.65), channel_id=1, source_target_pairs={{0,8},{8,16},{16,24},{24,32},{32,40},{40,48},{48,56},{1,9},{9,17},... | collective-permute-start | bytes 46088 | tf_op jit(solution)/shard_map/ppermute | solution.py:16
  14.7 4.5 %collective-permute-start.3 = (f32[3,10,1,128]{3,2,1,0:T(1,128)S(1)}, f32[3,10,1,128]{3,2,1,0:T(1,128)S(1)}, u32[]{:S(2)}, u32[]{:S(2)}) collective-permute-start(f32[3,10,1,128]{3,2,1,0:T(1,128)S(1)} %get-tuple-element.66), channel_id=1, source_target_pairs={{8,0},{16,8},{24,16},{32,24},{40,32},{48,40},{56,48},{9,1},{17,9},... | collective-permute-start | bytes 46088 | tf_op jit(solution)/shard_map/ppermute | solution.py:19
  19.4 10.7 %collective-permute-start.4 = (f32[3,10,18,1]{3,2,1,0:T(8,128)S(1)}, f32[3,10,18,1]{3,2,1,0:T(8,128)S(1)}, u32[]{:S(2)}, u32[]{:S(2)}) collective-permute-start(f32[3,10,18,1]{3,2,1,0:T(8,128)S(1)} %get-tuple-element.45), channel_id=1, source_target_pairs={{0,1},{1,2},{2,3},{3,4},{4,5},{5,6},{6,7},{8,9},{9,10},{10,11},{11... | collective-permute-start | bytes 6488 | tf_op jit(solution)/shard_map/ppermute | solution.py:16
  25.6 8.8 %collective-permute-start.5 = (f32[3,10,18,1]{3,2,1,0:T(8,128)S(1)}, f32[3,10,18,1]{3,2,1,0:T(8,128)S(1)}, u32[]{:S(2)}, u32[]{:S(2)}) collective-permute-start(f32[3,10,18,1]{3,2,1,0:T(8,128)S(1)} %get-tuple-element.46), channel_id=1, source_target_pairs={{1,0},{2,1},{3,2},{4,3},{5,4},{6,5},{7,6},{9,8},{10,9},{11,10},{12... | collective-permute-start | bytes 6488 | tf_op jit(solution)/shard_map/ppermute | solution.py:19
  36.3 5.3 %collective-permute-start.6 = (f32[3,1,16,128]{3,2,1,0:T(8,128)S(1)}, f32[3,1,16,128]{3,2,1,0:T(8,128)S(1)}, u32[]{:S(2)}, u32[]{:S(2)}) collective-permute-start(f32[3,1,16,128]{3,2,1,0:T(8,128)S(1)} %get-tuple-element.83), channel_id=1, source_target_pairs={{0,64},{64,128},{128,192},{192,256},{256,320},{320,384},{384,448},... | collective-permute-start | bytes 73736 | tf_op jit(solution)/shard_map/ppermute | solution.py:16
  40.3 6.4 %collective-permute-start.7 = (f32[3,1,16,128]{3,2,1,0:T(8,128)S(1)}, f32[3,1,16,128]{3,2,1,0:T(8,128)S(1)}, u32[]{:S(2)}, u32[]{:S(2)}) collective-permute-start(f32[3,1,16,128]{3,2,1,0:T(8,128)S(1)} %get-tuple-element.84), channel_id=1, source_target_pairs={{64,0},{128,64},{192,128},{256,192},{320,256},{384,320},{448,384},... | collective-permute-start | bytes 73736 | tf_op jit(solution)/shard_map/ppermute | solution.py:19
  46.8 4.5 %collective-permute-start.8 = (f32[3,10,1,128]{3,2,1,0:T(1,128)S(1)}, f32[3,10,1,128]{3,2,1,0:T(1,128)S(1)}, u32[]{:S(2)}, u32[]{:S(2)}) collective-permute-start(f32[3,10,1,128]{3,2,1,0:T(1,128)S(1)} %get-tuple-element.60), channel_id=1, source_target_pairs={{0,8},{8,16},{16,24},{24,32},{32,40},{40,48},{48,56},{1,9},{9,17},... | collective-permute-start | bytes 46088 | tf_op jit(solution)/shard_map/ppermute | solution.py:16
  50.0 5.1 %collective-permute-start.9 = (f32[3,10,1,128]{3,2,1,0:T(1,128)S(1)}, f32[3,10,1,128]{3,2,1,0:T(1,128)S(1)}, u32[]{:S(2)}, u32[]{:S(2)}) collective-permute-start(f32[3,10,1,128]{3,2,1,0:T(1,128)S(1)} %get-tuple-element.61), channel_id=1, source_target_pairs={{8,0},{16,8},{24,16},{32,24},{40,32},{48,40},{56,48},{9,1},{17,9},... | collective-permute-start | bytes 46088 | tf_op jit(solution)/shard_map/ppermute | solution.py:19
  55.3 8.5 %collective-permute-start.10 = (f32[3,10,18,1]{3,2,1,0:T(8,128)S(1)}, f32[3,10,18,1]{3,2,1,0:T(8,128)S(1)}, u32[]{:S(2)}, u32[]{:S(2)}) collective-permute-start(f32[3,10,18,1]{3,2,1,0:T(8,128)S(1)} %get-tuple-element.43), channel_id=1, source_target_pairs={{0,1},{1,2},{2,3},{3,4},{4,5},{5,6},{6,7},{8,9},{9,10},{10,11},{11... | collective-permute-start | bytes 6488 | tf_op jit(solution)/shard_map/ppermute | solution.py:16
  59.4 1.9 %copy-start.5 = (s32[256,1]{0,1:T(1,128)S(1)}, s32[256,1]{0,1:T(1,128)}, u32[]{:S(2)}) copy-start(s32[256,1]{0,1:T(1,128)} %param.16) | copy-start | bytes 3076
  59.4 8.8 %collective-permute-start.11 = (f32[3,10,18,1]{3,2,1,0:T(8,128)S(1)}, f32[3,10,18,1]{3,2,1,0:T(8,128)S(1)}, u32[]{:S(2)}, u32[]{:S(2)}) collective-permute-start(f32[3,10,18,1]{3,2,1,0:T(8,128)S(1)} %get-tuple-element.44), channel_id=1, source_target_pairs={{1,0},{2,1},{3,2},{4,3},{5,4},{6,5},{7,6},{9,8},{10,9},{11,10},{12... | collective-permute-start | bytes 6488 | tf_op jit(solution)/shard_map/ppermute | solution.py:19
  69.2 7.0 %collective-permute-start.12 = (f32[3,1,16,128]{3,2,1,0:T(8,128)S(1)}, f32[3,1,16,128]{3,2,1,0:T(8,128)S(1)}, u32[]{:S(2)}, u32[]{:S(2)}) collective-permute-start(f32[3,1,16,128]{3,2,1,0:T(8,128)S(1)} %get-tuple-element.81), channel_id=1, source_target_pairs={{0,64},{64,128},{128,192},{192,256},{256,320},{320,384},{384,448},... | collective-permute-start | bytes 73736 | tf_op jit(solution)/shard_map/ppermute | solution.py:16
  74.1 4.9 %collective-permute-start.13 = (f32[3,1,16,128]{3,2,1,0:T(8,128)S(1)}, f32[3,1,16,128]{3,2,1,0:T(8,128)S(1)}, u32[]{:S(2)}, u32[]{:S(2)}) collective-permute-start(f32[3,1,16,128]{3,2,1,0:T(8,128)S(1)} %get-tuple-element.82), channel_id=1, source_target_pairs={{64,0},{128,64},{192,128},{256,192},{320,256},{384,320},{448,384},... | collective-permute-start | bytes 73736 | tf_op jit(solution)/shard_map/ppermute | solution.py:19
  79.0 6.3 %collective-permute-start.14 = (f32[3,10,1,128]{3,2,1,0:T(1,128)S(1)}, f32[3,10,1,128]{3,2,1,0:T(1,128)S(1)}, u32[]{:S(2)}, u32[]{:S(2)}) collective-permute-start(f32[3,10,1,128]{3,2,1,0:T(1,128)S(1)} %get-tuple-element.55), channel_id=1, source_target_pairs={{0,8},{8,16},{16,24},{24,32},{32,40},{40,48},{48,56},{1,9},{9,17},... | collective-permute-start | bytes 46088 | tf_op jit(solution)/shard_map/ppermute | solution.py:16
  83.8 4.8 %collective-permute-start.15 = (f32[3,10,1,128]{3,2,1,0:T(1,128)S(1)}, f32[3,10,1,128]{3,2,1,0:T(1,128)S(1)}, u32[]{:S(2)}, u32[]{:S(2)}) collective-permute-start(f32[3,10,1,128]{3,2,1,0:T(1,128)S(1)} %get-tuple-element.56), channel_id=1, source_target_pairs={{8,0},{16,8},{24,16},{32,24},{40,32},{48,40},{56,48},{9,1},{17,9},... | collective-permute-start | bytes 46088 | tf_op jit(solution)/shard_map/ppermute | solution.py:19
  88.8 8.5 %collective-permute-start.16 = (f32[3,10,18,1]{3,2,1,0:T(8,128)S(1)}, f32[3,10,18,1]{3,2,1,0:T(8,128)S(1)}, u32[]{:S(2)}, u32[]{:S(2)}) collective-permute-start(f32[3,10,18,1]{3,2,1,0:T(8,128)S(1)} %get-tuple-element.41), channel_id=1, source_target_pairs={{0,1},{1,2},{2,3},{3,4},{4,5},{5,6},{6,7},{8,9},{9,10},{10,11},{11... | collective-permute-start | bytes 6488 | tf_op jit(solution)/shard_map/ppermute | solution.py:16
  92.9 8.8 %collective-permute-start.17 = (f32[3,10,18,1]{3,2,1,0:T(8,128)S(1)}, f32[3,10,18,1]{3,2,1,0:T(8,128)S(1)}, u32[]{:S(2)}, u32[]{:S(2)}) collective-permute-start(f32[3,10,18,1]{3,2,1,0:T(8,128)S(1)} %get-tuple-element.42), channel_id=1, source_target_pairs={{1,0},{2,1},{3,2},{4,3},{5,4},{6,5},{7,6},{9,8},{10,9},{11,10},{12... | collective-permute-start | bytes 6488 | tf_op jit(solution)/shard_map/ppermute | solution.py:19
  102.7 31.0 %copy-start = (f32[3,8,16,128]{3,2,1,0:T(8,128)}, f32[3,8,16,128]{3,2,1,0:T(8,128)S(1)}, u32[]{:S(2)}) copy-start(f32[3,8,16,128]{3,2,1,0:T(8,128)S(1)} %fusion.14) | copy-start | bytes 589828
  102.7 5.0 %collective-permute-start.18 = (f32[3,1,16,128]{3,2,1,0:T(8,128)S(1)}, f32[3,1,16,128]{3,2,1,0:T(8,128)S(1)}, u32[]{:S(2)}, u32[]{:S(2)}) collective-permute-start(f32[3,1,16,128]{3,2,1,0:T(8,128)S(1)} %get-tuple-element.79), channel_id=1, source_target_pairs={{0,64},{64,128},{128,192},{192,256},{256,320},{320,384},{384,448},... | collective-permute-start | bytes 73736 | tf_op jit(solution)/shard_map/ppermute | solution.py:16
  106.4 4.6 %collective-permute-start.19 = (f32[3,1,16,128]{3,2,1,0:T(8,128)S(1)}, f32[3,1,16,128]{3,2,1,0:T(8,128)S(1)}, u32[]{:S(2)}, u32[]{:S(2)}) collective-permute-start(f32[3,1,16,128]{3,2,1,0:T(8,128)S(1)} %get-tuple-element.80), channel_id=1, source_target_pairs={{64,0},{128,64},{192,128},{256,192},{320,256},{384,320},{448,384},... | collective-permute-start | bytes 73736 | tf_op jit(solution)/shard_map/ppermute | solution.py:19
  111.0 5.0 %copy-start.8 = (s32[256]{0:T(256)S(1)}, s32[256]{0:T(256)}, u32[]{:S(2)}) copy-start(s32[256]{0:T(256)} %param.15) | copy-start | bytes 3076
  111.0 5.0 %collective-permute-start.20 = (f32[3,10,1,128]{3,2,1,0:T(1,128)S(1)}, f32[3,10,1,128]{3,2,1,0:T(1,128)S(1)}, u32[]{:S(2)}, u32[]{:S(2)}) collective-permute-start(f32[3,10,1,128]{3,2,1,0:T(1,128)S(1)} %get-tuple-element.50), channel_id=1, source_target_pairs={{0,8},{8,16},{16,24},{24,32},{32,40},{40,48},{48,56},{1,9},{9,17},... | collective-permute-start | bytes 46088 | tf_op jit(solution)/shard_map/ppermute | solution.py:16
  114.7 4.5 %collective-permute-start.21 = (f32[3,10,1,128]{3,2,1,0:T(1,128)S(1)}, f32[3,10,1,128]{3,2,1,0:T(1,128)S(1)}, u32[]{:S(2)}, u32[]{:S(2)}) collective-permute-start(f32[3,10,1,128]{3,2,1,0:T(1,128)S(1)} %get-tuple-element.51), channel_id=1, source_target_pairs={{8,0},{16,8},{24,16},{32,24},{40,32},{48,40},{56,48},{9,1},{17,9},... | collective-permute-start | bytes 46088 | tf_op jit(solution)/shard_map/ppermute | solution.py:19
  119.4 9.0 %collective-permute-start.22 = (f32[3,10,18,1]{3,2,1,0:T(8,128)S(1)}, f32[3,10,18,1]{3,2,1,0:T(8,128)S(1)}, u32[]{:S(2)}, u32[]{:S(2)}) collective-permute-start(f32[3,10,18,1]{3,2,1,0:T(8,128)S(1)} %get-tuple-element.39), channel_id=1, source_target_pairs={{0,1},{1,2},{2,3},{3,4},{4,5},{5,6},{6,7},{8,9},{9,10},{10,11},{11... | collective-permute-start | bytes 6488 | tf_op jit(solution)/shard_map/ppermute | solution.py:16
  124.0 2.0 %copy-start.9 = (s32[256]{0:T(256)S(1)}, s32[256]{0:T(256)}, u32[]{:S(2)}) copy-start(s32[256]{0:T(256)} %param.17) | copy-start | bytes 3076
  124.0 8.8 %collective-permute-start.23 = (f32[3,10,18,1]{3,2,1,0:T(8,128)S(1)}, f32[3,10,18,1]{3,2,1,0:T(8,128)S(1)}, u32[]{:S(2)}, u32[]{:S(2)}) collective-permute-start(f32[3,10,18,1]{3,2,1,0:T(8,128)S(1)} %get-tuple-element.40), channel_id=1, source_target_pairs={{1,0},{2,1},{3,2},{4,3},{5,4},{6,5},{7,6},{9,8},{10,9},{11,10},{12... | collective-permute-start | bytes 6488 | tf_op jit(solution)/shard_map/ppermute | solution.py:19
  133.8 1.8 copy-start.11
  133.8 1.8 copy-start.12
  160.7 14.0 %all-to-all-start.1 = ((f32[1,64,8]{2,0,1:T(1,128)}), f32[1,64,8]{2,0,1:T(1,128)S(1)}, u32[]{:S(2)}, u32[]{:S(2)}) async-start(f32[1,64,8]{2,0,1:T(1,128)} %bitcast.50), calls=%async_computation.1 | async-start | bytes 65536 | tf_op jit(solution)/shard_map/all_to_all | solution.py:111
  178.0 2.0 %copy-start.7 = (f32[256]{0:T(256)}, f32[256]{0:T(256)S(1)}, u32[]{:S(2)}) copy-start(f32[256]{0:T(256)S(1)} %gather_fusion.1) | copy-start | bytes 3076
  (8 other events, 7.9 us)
where the time goes:
time: 182 us; the launch traced here: 181 us
  starting transfers between devices  73.9 us (41%)
  waiting for transfers between devices  63.7 us (35%)
  blocking collectives  19.6 us (11%)
  local copies, waits for them, and re-layouts  13.7 us (8%)
  other arithmetic  7.48 us (4%)
    ppermute x12, starting transfers between devices, with_halo(): lax.ppermute(lax.slice_in_dim(block, block.shape[dim] - width, None, axis...  51.2 us
    ppermute x12, waiting for transfers between devices, with_halo(): lax.ppermute(lax.slice_in_dim(block, 0, width, axis=dim), axis, backward)  45.1 us
    all_to_all x1, blocking collectives, on_device(): lax.all_to_all(outgoing, ('gy', 'gz'), split_axis=1, concat_axis=1, tiled...  19.6 us
    ppermute x12, starting transfers between devices, with_halo(): lax.ppermute(lax.slice_in_dim(block, 0, width, axis=dim), axis, backward)  18 us
    ppermute x12, waiting for transfers between devices, with_halo(): lax.ppermute(lax.slice_in_dim(block, block.shape[dim] - width, None, axis...  9.34 us
    all_to_all x1, waiting for transfers between devices, on_device(): lax.all_to_all(answer[None], ('gy', 'gz'), split_axis=1, concat_axis=1, t...  9.29 us
    all_to_all x1, starting transfers between devices, on_device(): lax.all_to_all(answer[None], ('gy', 'gz'), split_axis=1, concat_axis=1, t...  4.71 us
    unnamed x30, local copies, waits for them, and re-layouts  3.73 us
  transfers between devices with their start and end apart: 25, of which 17 were waited for; matrix products, arithmetic and copies ran while one was open for 1% of the time, Pallas kernels for 0%

commit v1 on v0

v1 whole, which is shorter than its diff:
```python
import jax
import jax.numpy as jnp
from jax import lax
from jax.experimental import pallas as pl
from jax.experimental.pallas import tpu as pltpu
from jax.sharding import PartitionSpec as P

MESH = pl.DeviceIdType.MESH
F32 = jnp.float32
BF16 = jnp.bfloat16
N = 8
W = 4
CX, CY, CZ = 8, 16, 128
EX, EY = CX + 2 * W, CY + 2 * W
PORTS = 256
GROUPS = 8
NPAR = 5


def pieces(value):
    high = value.astype(BF16).astype(F32)
    rest = value - high
    mid = rest.astype(BF16).astype(F32)
    return high, mid, rest - mid


def dot_nt(a, b):
    return lax.dot_general(a, b, (((1,), (1,)), ((), ())), preferred_element_type=F32)


def dot_nn(a, b):
    return lax.dot_general(a, b, (((1,), (0,)), ((), ())), preferred_element_type=F32)


def three(dot, value, other):
    rows = value.shape[0]
    out = dot(jnp.concatenate(pieces(value), axis=0).astype(BF16), other)
    return (out[:rows] + out[rows : 2 * rows]) + out[2 * rows :]


def up_z(main, halo, lane):
    rm, rh = pltpu.roll(main, CZ - 1, 1), pltpu.roll(halo, CZ - 1, 1)
    return jnp.where(lane == CZ - 1, rh, rm), jnp.where(lane == CZ - 1, rm, rh)


def down_z(main, halo, lane):
    rm, rh = pltpu.roll(main, 1, 1), pltpu.roll(halo, 1, 1)
    return jnp.where(lane == 0, rh, rm), jnp.where(lane == 0, rm, rh)


def up_y(v):
    return pltpu.roll(v, EY - 1, 0)


def down_y(v):
    return pltpu.roll(v, 1, 0)


def substep(now, now_h, old, old_h, cou, cou_h, low, high, last):
    lane = lax.broadcasted_iota(jnp.int32, (EY, CZ), 1)

    def curls(x):
        vx, vy, vz = now[0, x], now[1, x], now[2, x]
        vxh, vyh, vzh = now_h[0, x], now_h[1, x], now_h[2, x]
        vxu, vxuh = up_z(vx, vxh, lane)
        gy = (vxu - vx) - (now[2, x + 1] - vz)
        gyh = (vxuh - vxh) - (now_h[2, x + 1] - vzh)
        gz = (now[1, x + 1] - vy) - (up_y(vx) - vx)
        gzh = (now_h[1, x + 1] - vyh) - (up_y(vxh) - vxh)
        return gy, gyh, gz, gzh

    def body(x, carry):
        gyp, gyph, gzp, gzph = carry
        vx, vy, vz = now[0, x], now[1, x], now[2, x]
        vxh, vyh, vzh = now_h[0, x], now_h[1, x], now_h[2, x]
        gy, gyh, gz, gzh = curls(x)
        vyu, vyuh = up_z(vy, vyh, lane)
        gx = (up_y(vz) - vz) - (vyu - vy)
        gxh = (up_y(vzh) - vzh) - (vyuh - vyh)
        gxd, gxdh = down_z(gx, gxh, lane)
        gyd, gydh = down_z(gy, gyh, lane)
        c = cou[x]
        kx = (gz - down_y(gz)) - (gy - gyd)
        ky = (gx - gxd) - (gz - gzp)
        kz = (gy - gyp) - (gx - down_y(gx))
        old[0, x] = 2.0 * vx - old[0, x] - c * kx
        old[1, x] = 2.0 * vy - old[1, x] - c * ky
        old[2, x] = 2.0 * vz - old[2, x] - c * kz
        if not last:
            ch = cou_h[x]
            kxh = (gzh - down_y(gzh)) - (gyh - gydh)
            kyh = (gxh - gxdh) - (gzh - gzph)
            kzh = (gyh - gyph) - (gxh - down_y(gxh))
            old_h[0, x] = 2.0 * vxh - old_h[0, x] - ch * kxh
            old_h[1, x] = 2.0 * vyh - old_h[1, x] - ch * kyh
            old_h[2, x] = 2.0 * vzh - old_h[2, x] - ch * kzh
        return gy, gyh, gz, gzh

    lax.fori_loop(low, high, body, curls(low - 1))


def kernel(
    e_ref,
    ep_ref,
    co_ref,
    cell_ref,
    route_ref,
    group_ref,
    gain_ref,
    drive_ref,
    bias_ref,
    couple_ref,
    next_ref,
    last_ref,
    cur_ref,
    own,
    a,
    ah,
    b,
    bh,
    c,
    ch,
    pz,
    px,
    py,
    pc,
    qz,
    qx,
    qy,
    qc,
    iport,
    fport,
    ownpar,
    ownsam,
    par,
    sam,
    node,
    finz,
    curv,
    drain,
    lsem,
    hsend,
    hrecv,
    ysend,
    yrecv,
    xsend,
    xrecv,
    tsem,
    ssend,
    srecv,
):
    gx, gy, gz = lax.axis_index("gx"), lax.axis_index("gy"), lax.axis_index("gz")
    me = gz * N + gy

    def near(dx, dy, dz):
        return (lax.rem(gx + N + dx, N), lax.rem(gy + N + dy, N), lax.rem(gz + N + dz, N))

    barrier = pltpu.get_barrier_semaphore()

    for dx in (-1, 1):
        for dy in (-1, 0, 1):
            for dz in (-1, 0, 1):
                pl.semaphore_signal(barrier, inc=1, device_id=near(dx, dy, dz), device_id_type=MESH)

    def greet(k, _):
        t = lax.rem(me + k, N * N)
        pl.semaphore_signal(
            barrier, inc=1, device_id=(gx, lax.rem(t, N), t // N), device_id_type=MESH
        )
        return 0

    lax.fori_loop(1, N * N, greet, 0)

    inner = (pl.ds(W, CX), pl.ds(W, CY))
    local = [
        (e_ref, own.at[0:3]),
        (ep_ref, own.at[3:6]),
        (co_ref, own.at[6]),
        (cell_ref, iport.at[0]),
        (route_ref, iport.at[1]),
        (group_ref, iport.at[2]),
        (gain_ref, fport.at[0]),
        (drive_ref, fport.at[1]),
        (bias_ref, fport.at[2]),
        (couple_ref, fport.at[3]),
        (e_ref, a.at[:, inner[0], inner[1]]),
        (ep_ref, b.at[:, inner[0], inner[1]]),
        (co_ref, c.at[inner[0], inner[1]]),
    ]
    local = [pltpu.make_async_copy(s, d, lsem.at[i]) for i, (s, d) in enumerate(local)]
    for copy in local:
        copy.start()
    for copy in local[:3]:
        copy.wait()

    lane = lax.broadcasted_iota(jnp.int32, (CZ, CZ), 1)
    packed = jnp.zeros((CZ, CZ), F32)
    for f in range(7):
        rolled = pltpu.roll(own[f].reshape(CZ, CZ), W + 8 * f, 1)
        packed = jnp.where(lane // 8 == f, rolled, packed)
    packed = packed.T
    lane8 = lax.broadcasted_iota(jnp.int32, (8, CZ), 1)
    slot = lane8 % CY // W
    rows = [packed[8 * f : 8 * f + 8] for f in range(7)]
    for f in range(7):
        pz[f] = rows[f]

    def turn(v, shift):
        shift = shift % CZ
        return v if shift == 0 else pltpu.roll(v, shift, 1)

    def quarters(group, top):
        out = turn(group[0], -12 if top else 0)
        for j in range(1, len(group)):
            out = jnp.where(slot == j, turn(group[j], 4 * j - (12 if top else 0)), out)
        return out

    halves = []
    for top in (0, 1):
        tiles = []
        for j in range(4):
            if j == 3:
                tile = turn(rows[3], 64 * top)
            elif top:
                tile = jnp.where(lane8 < 64, turn(rows[j], 64), rows[j + 4])
            else:
                tile = jnp.where(lane8 < 64, rows[j], turn(rows[j + 4], 64))
            px[top, j] = tile
            tiles.append(tile)
        halves.append(tiles)
    for top in (0, 1):
        py[top, 0] = quarters(rows[0:4], top)
        py[top, 1] = quarters(rows[4:7], top)
        for xt in (0, 1):
            pc[xt, top] = quarters(halves[xt], top)

    for copy in local[3:]:
        copy.wait()
    route = iport[1]
    at64 = lax.broadcasted_iota(jnp.int32, (64, PORTS), 0) == route
    earlier = lax.broadcasted_iota(jnp.int32, (PORTS, PORTS), 0) < lax.broadcasted_iota(
        jnp.int32, (PORTS, PORTS), 1
    )
    count = dot_nn(
        jnp.where(at64, 1.0, 0.0).astype(BF16), jnp.where(earlier, 1.0, 0.0).astype(BF16)
    )
    rank = jnp.sum(jnp.where(at64, count, 0.0), axis=0, keepdims=True).astype(jnp.int32)
    slot_lane = route + 64 * (rank % 2)
    slot_row = rank // 2
    iota128 = lax.broadcasted_iota(jnp.int32, (CZ, PORTS), 0)
    to_lane = jnp.where(iota128 == slot_lane, 1.0, 0.0).astype(BF16)
    iota8 = lax.broadcasted_iota(jnp.int32, (8, PORTS), 0)
    in_row = iota8 % 4 == slot_row
    values = [fport[0], fport[1], fport[2], fport[3], iport[2].astype(F32) + 1.0]
    stacked = jnp.concatenate(
        [
            jnp.where(in_row, jnp.where(iota8 < 4, values[2 * i], values[min(2 * i + 1, 4)]), 0.0)
            for i in range(3)
        ],
        axis=0,
    )
    slots = three(dot_nt, stacked, to_lane)
    for i in range(NPAR):
        ownpar[i] = slots[4 * i : 4 * i + 4]
    cell = iport[0]
    row_hot = iota128 == cell // CZ
    z_hot = iota128 == cell % CZ

    pl.semaphore_wait(barrier, N * N - 1 + 18)

    def span(d, width, size):
        if d == 0:
            return pl.ds(0, size), pl.ds(W, size)
        if d > 0:
            return pl.ds(size - width, width), pl.ds(W - width, width)
        return pl.ds(0, width), pl.ds(W + size, width)

    halo = []

    def send(src, dst, d):
        i = len(halo)
        copy = pltpu.make_async_remote_copy(
            src_ref=src,
            dst_ref=dst,
            send_sem=hsend.at[i],
            recv_sem=hrecv.at[i],
            device_id=near(*d),
            device_id_type=MESH,
        )
        copy.start()
        halo.append(copy)

    flat = [(1, 0), (-1, 0), (1, 1), (1, -1), (-1, 1), (-1, -1), (0, 1), (0, -1)]
    for dx, dy in flat:
        sx4, tx4 = span(dx, W, CX)
        sy4, ty4 = span(dy, W, CY)
        sx3, tx3 = span(dx, W - 1, CX)
        sy3, ty3 = span(dy, W - 1, CY)
        send(own.at[0:3, sx4, sy4], a.at[:, tx4, ty4], (dx, dy, 0))
        send(own.at[3:6, sx3, sy3], b.at[:, tx3, ty3], (dx, dy, 0))
        send(own.at[6, sx3, sy3], c.at[tx3, ty3], (dx, dy, 0))
    n_flat = len(halo)
    for dz in (1, -1):
        part = pl.ds(0, W) if dz > 0 else pl.ds(W, W)
        send(pz.at[:, part], qz.at[:, part], (0, 0, dz))
        for d in (1, -1):
            mine, theirs = (1, 0) if d > 0 else (0, 1)
            send(px.at[mine, :, part], qx.at[theirs, :, part], (d, 0, dz))
            send(py.at[mine, :, part], qy.at[theirs, :, part], (0, d, dz))
            for dy in (1, -1):
                mine_y, theirs_y = (1, 0) if dy > 0 else (0, 1)
                send(pc.at[mine, mine_y, part], qc.at[theirs, theirs_y, part], (d, dy, dz))

    half = pl.ds(4 * lax.rem(gy, 2), 4)
    spread_y = []
    for k in range(1, N):
        copy = pltpu.make_async_remote_copy(
            src_ref=ownpar,
            dst_ref=par.at[gz, gy // 2, :, half],
            send_sem=ysend.at[k - 1],
            recv_sem=yrecv.at[k - 1],
            device_id=(gx, lax.rem(gy + k, N), gz),
            device_id_type=MESH,
        )
        copy.start()
        spread_y.append(copy)
    own_par = pltpu.make_async_copy(ownpar, par.at[gz, gy // 2, :, half], lsem.at[0])
    own_par.start()

    for copy in halo[n_flat:]:
        copy.wait_recv()
    low_ok = jnp.where(gz > 0, 1, 0)
    high_ok = jnp.where(gz < N - 1, 1, 0)
    keep = jnp.where(lane < CZ // 2, high_ok, low_ok) == 1

    def unpack(tiles, store):
        block = jnp.concatenate(tiles + [jnp.zeros((CZ - 56, CZ), F32)], axis=0).T
        for f in range(7):
            value = jnp.where(keep, pltpu.roll(block, (CZ - 8 * f - W) % CZ, 1), 0.0)
            ref = (ah, bh, ch)[f // 3]
            store(ref if f == 6 else ref.at[f % 3], value)

    def store_own(ref, value):
        ref[W : W + CX, W : W + CY] = value.reshape(CX, CY, CZ)

    def store_x(ref, value):
        value = value.reshape(CX, CY, CZ)
        ref[0:W, W : W + CY] = value[:W]
        ref[W + CX :, W : W + CY] = value[W:]

    def store_y(ref, value):
        value = value.reshape(CX, 4, W, CZ)
        ref[W : W + CX, 0:W] = value[:, 0]
        ref[W : W + CX, W + CY :] = value[:, 1]
        ref[0:W, 0:W] = value[:W, 2]
        ref[W + CX :, 0:W] = value[W:, 2]
        ref[0:W, W + CY :] = value[:W, 3]
        ref[W + CX :, W + CY :] = value[W:, 3]

    unpack([qz[f] for f in range(7)], store_own)
    tiles = []
    for f in range(7):
        h, j = f // 4, f % 4
        if h == 0:
            tiles.append(jnp.where(lane8 < 64, qx[0, j], pltpu.roll(qx[1, j], 64, 1)))
        else:
            tiles.append(jnp.where(lane8 < 64, pltpu.roll(qx[0, j], 64, 1), qx[1, j]))
    unpack(tiles, store_x)
    tiles = []
    for f in range(7):
        h, j = f // 4, f % 4
        tile = jnp.where(slot == 0, turn(qy[0, h], -4 * j), turn(qy[1, h], 4 - 4 * j))
        for s in (0, 1):
            shift = 8 + 4 * s - 4 * j - 64 * h
            corner = jnp.where(lane8 < 64, turn(qc[0, s], shift), turn(qc[1, s], shift + 64))
            tile = jnp.where(slot == 2 + s, corner, tile)
        tiles.append(tile)
    unpack(tiles, store_y)

    own_par.wait()
    for copy in spread_y:
        copy.wait_recv()
    spread_x = []
    for k in range(1, 4):
        copy = pltpu.make_async_remote_copy(
            src_ref=par.at[gz],
            dst_ref=par.at[gz],
            send_sem=xsend.at[k - 1],
            recv_sem=xrecv.at[k - 1],
            device_id=(gx, gy, lax.rem(gz + 2 * k, N)),
            device_id_type=MESH,
        )
        copy.start()
        spread_x.append(copy)

    for copy in halo[:n_flat]:
        copy.wait_recv()

    def clear(xs, ys):
        for ref in (a, ah, b, bh):
            ref[:, xs, ys] = jnp.zeros_like(ref[:, xs, ys])
        for ref in (c, ch):
            ref[xs, ys] = jnp.zeros_like(ref[xs, ys])

    @pl.when(gx == 0)
    def _():
        clear(slice(0, W), slice(0, EY))

    @pl.when(gx == N - 1)
    def _():
        clear(slice(W + CX, EX), slice(0, EY))

    @pl.when(gy == 0)
    def _():
        clear(slice(0, EX), slice(0, W))

    @pl.when(gy == N - 1)
    def _():
        clear(slice(0, EX), slice(W + CY, EY))

    substep(a, ah, b, bh, c, ch, 1, EX - 1, False)
    substep(b, bh, a, ah, c, ch, 2, EX - 2, False)
    substep(a, ah, b, bh, c, ch, 3, EX - 3, False)
    out_last = pltpu.make_async_copy(b.at[:, inner[0], inner[1]], last_ref, lsem.at[1])
    out_last.start()
    substep(b, bh, a, ah, c, ch, 4, EX - 4, True)
    out_next = pltpu.make_async_copy(
        a.at[0:2, inner[0], inner[1]], next_ref.at[0:2], lsem.at[2]
    )
    out_next.start()

    ez = a[2, W : W + CX, W : W + CY].reshape(CZ, CZ)
    row_one = jnp.where(row_hot, 1.0, 0.0).astype(BF16)
    picked = three(dot_nn, ez.T, row_one)
    sample = jnp.sum(jnp.where(z_hot, picked, 0.0), axis=0, keepdims=True)
    sample8 = three(dot_nt, jnp.where(in_row, sample, 0.0), to_lane)
    ownsam[...] = sample8[0:4]
    for k in range(1, N * N):
        t = lax.rem(me + k, N * N)
        pltpu.make_async_remote_copy(
            src_ref=ownsam,
            dst_ref=sam.at[gz, gy // 2, half],
            send_sem=ssend,
            recv_sem=srecv,
            device_id=(gx, lax.rem(t, N), t // N),
            device_id_type=MESH,
        ).start()
    own_sam = pltpu.make_async_copy(ownsam, sam.at[gz, gy // 2, half], lsem.at[0])
    own_sam.start()

    for copy in spread_x:
        copy.wait_recv()
    core = lax.rem(gz, 2)
    twins = []
    for i in range(4):
        copy = pltpu.make_async_remote_copy(
            src_ref=par.at[2 * i + core],
            dst_ref=par.at[2 * i + core],
            send_sem=tsem.at[0, i],
            recv_sem=tsem.at[1, i],
            device_id=(gx, gy, gz + 1 - 2 * core),
            device_id_type=MESH,
        )
        copy.start()
        twins.append(copy)
    for copy in twins:
        copy.wait_recv()
    own_sam.wait()
    pltpu.make_async_copy(drain, drain, srecv).wait()

    sub = lax.broadcasted_iota(jnp.int32, (8, CZ), 0)

    def totals(first):
        def add(i, acc):
            for j in range(N // 2):
                volt = sam[i, j] if first else node[i, j]
                s = jnp.tanh(volt)
                grp = par[i, j, 4]
                acc = tuple(
                    acc[g] + jnp.where(grp == float(g + 1), s, 0.0) for g in range(GROUPS)
                )
            return acc

        acc = lax.fori_loop(0, N, add, tuple(jnp.zeros((8, CZ), F32) for _ in range(GROUPS)))
        total = jnp.zeros((8, CZ), F32)
        for g in range(GROUPS):
            total = jnp.where(sub == g, jnp.sum(acc[g], axis=0, keepdims=True), total)
        return total + pltpu.roll(total, 64, 1)

    def newton(volt, sample, gain, drive, bias, couple, grp, total):
        s = jnp.tanh(volt)
        shared = jnp.zeros_like(volt)
        for g in range(GROUPS):
            shared = jnp.where(grp == float(g + 1), total[g : g + 1], shared)
        resid = (1.0 + gain) * volt - sample - bias + drive * s + couple * shared
        slope = 1.0 + gain + (drive + couple) * (1.0 - s * s)
        return volt - resid / slope

    mine = sample8
    my = [ownpar[i] for i in range(NPAR)]
    my = [jnp.concatenate([v, v], axis=0) for v in my]
    volt = mine
    for iterate in range(3):
        total = totals(iterate == 0)
        volt = newton(volt, mine, *my, total)
        if iterate < 2:

            def move(i, _):
                for j in range(N // 2):
                    start = sam[i, j]
                    now = start if iterate == 0 else node[i, j]
                    node[i, j] = newton(
                        now, start, *[par[i, j, p] for p in range(NPAR)], total
                    )
                return 0

            lax.fori_loop(0, N, move, 0)
    current = my[0] * (volt - mine)

    spread = three(dot_nn, current, to_lane)
    port = jnp.sum(jnp.where(in_row & (iota8 < 4), spread, 0.0), axis=0, keepdims=True)
    curv[...] = port
    out_cur = pltpu.make_async_copy(curv, cur_ref, lsem.at[3])
    out_cur.start()
    z_one = jnp.where(z_hot, 1.0, 0.0).astype(BF16)
    extra = three(dot_nt, jnp.where(row_hot, port, 0.0), z_one)
    finz[...] = (a[2, W : W + CX, W : W + CY].reshape(CZ, CZ) + extra).reshape(CX, CY, CZ)
    out_z = pltpu.make_async_copy(finz, next_ref.at[2], lsem.at[4])
    out_z.start()
    for copy in (out_last, out_next, out_cur, out_z):
        copy.wait()
    for copy in halo + spread_y + spread_x + twins:
        copy.wait_send()
    pltpu.make_async_copy(drain, drain, ssend).wait()


def on_device(e, ep, co, cell, route, group, gain, drive, bias, couple):
    line = lambda v: v.reshape(1, PORTS)
    any_spec = pl.BlockSpec(memory_space=pl.ANY)
    dma = pltpu.SemaphoreType.DMA
    ext, ext1 = pltpu.VMEM((3, EX, EY, CZ), F32), pltpu.VMEM((EX, EY, CZ), F32)
    electric, last, current = pl.pallas_call(
        kernel,
        out_shape=(
            jax.ShapeDtypeStruct((3, CX, CY, CZ), F32),
            jax.ShapeDtypeStruct((3, CX, CY, CZ), F32),
            jax.ShapeDtypeStruct((1, PORTS), F32),
        ),
        in_specs=[any_spec] * 10,
        out_specs=(any_spec,) * 3,
        scratch_shapes=[
            pltpu.VMEM((7, CX, CY, CZ), F32),
            ext,
            ext,
            ext,
            ext,
            ext1,
            ext1,
            pltpu.VMEM((7, 8, CZ), F32),
            pltpu.VMEM((2, 4, 8, CZ), F32),
            pltpu.VMEM((2, 2, 8, CZ), F32),
            pltpu.VMEM((2, 2, 8, CZ), F32),
            pltpu.VMEM((7, 8, CZ), F32),
            pltpu.VMEM((2, 4, 8, CZ), F32),
            pltpu.VMEM((2, 2, 8, CZ), F32),
            pltpu.VMEM((2, 2, 8, CZ), F32),
            pltpu.VMEM((3, 1, PORTS), jnp.int32),
            pltpu.VMEM((4, 1, PORTS), F32),
            pltpu.VMEM((NPAR, 4, CZ), F32),
            pltpu.VMEM((4, CZ), F32),
            pltpu.VMEM((N, N // 2, NPAR, 8, CZ), F32),
            pltpu.VMEM((N, N // 2, 8, CZ), F32),
            pltpu.VMEM((N, N // 2, 8, CZ), F32),
            pltpu.VMEM((CX, CY, CZ), F32),
            pltpu.VMEM((1, PORTS), F32),
            pltpu.VMEM((N * N - 1, 4, CZ), F32),
            dma((13,)),
            dma((42,)),
            dma((42,)),
            dma((N - 1,)),
            dma((N - 1,)),
            dma((3,)),
            dma((3,)),
            dma((2, 4)),
            dma,
            dma,
        ],
        compiler_params=pltpu.CompilerParams(
            collective_id=0, has_side_effects=True, vmem_limit_bytes=32 * 1024 * 1024
        ),
    )(e, ep, co, line(cell), line(route), line(group), line(gain), line(drive), line(bias), line(couple))
    return electric, last, current.reshape(PORTS)


def solution(mesh):
    field = P(None, "gx", "gy", "gz")
    port = P(("gx", "gy", "gz"))
    placed = (
        field,
        field,
        P("gx", "gy", "gz"),
        port,
        P(("gx", "gy", "gz"), None),
        port,
        port,
        port,
        port,
        port,
    )
    return jax.shard_map(
        on_device,
        mesh=mesh,
        in_specs=placed,
        out_specs=(field, field, port),
        check_vma=False,
    )
```

time: 182 us -> 51 us (0.28)
  starting transfers between devices: 73.9 us -> 0 us
  waiting for transfers between devices: 63.7 us -> 0 us
  Pallas kernels: 0 us -> 44.7 us
  blocking collectives: 19.6 us -> 0 us
  local copies, waits for them, and re-layouts: 13.7 us -> 5.33 us
  other arithmetic: 7.48 us -> 0 us
    ppermute x24 -> x0, starting transfers between devices: 69.2 us -> none  [the longest x12 51.2 us: with_halo(): lax.ppermute(lax.slice_in_dim(block, block.shape[dim] - width, None, axis...]
    ppermute x24 -> x0, waiting for transfers between devices: 54.4 us -> none  [the longest x12 45.1 us: with_halo(): lax.ppermute(lax.slice_in_dim(block, 0, width, axis=dim), axis, backward)]
    pallas_call x0 -> x1, Pallas kernels: none -> 44.7 us  [on_device(): pl.pallas_call(kernel, out_shape=(jax.ShapeDtypeStruct((3, CX, CY, CZ), F...]
    all_to_all x1 -> x0, blocking collectives: 19.6 us -> none  [on_device(): lax.all_to_all(outgoing, ('gy', 'gz'), split_axis=1, concat_axis=1, tiled...]
    all_to_all x1 -> x0, waiting for transfers between devices: 9.29 us -> none  [on_device(): lax.all_to_all(answer[None], ('gy', 'gz'), split_axis=1, concat_axis=1, t...]
    all_to_all x1 -> x0, starting transfers between devices: 4.71 us -> none  [on_device(): lax.all_to_all(answer[None], ('gy', 'gz'), split_axis=1, concat_axis=1, t...]
    gather x2 -> x0, local copies, waits for them, and re-layouts: 3.67 us -> none  [the longest x1 1.95 us: on_device(): current = returned[target]]
    slice x11 -> x0, local copies, waits for them, and re-layouts: 2.16 us -> none  [the longest x1 0.77 us: with_halo(): lax.slice_in_dim(block, 0, width, axis=dim)]
  transfers between devices with their start and end apart: 25 -> 0, of which waited for: 17 -> 0; matrix products, arithmetic and copies ran while one was open for 1% -> 0% of each run, Pallas kernels for 0% -> 0%
where the time goes in v1:
time: 51 us; the launch traced here: 50.7 us
  Pallas kernels  44.7 us (88%)
  local copies, waits for them, and re-layouts  5.33 us (10%)
  between operations  0.71 us (1%)
    pallas_call x1, Pallas kernels, on_device(): pl.pallas_call(kernel, out_shape=(jax.ShapeDtypeStruct((3, CX, CY, CZ), F...  44.7 us
    unnamed x23, local copies, waits for them, and re-layouts  5.33 us

profile of v1, /device:TPU:1, one launch (start us, length us, event | category | flops | bytes accessed | tf_op | source)
XLA Modules:
  0.0 50.7 jit_solution(10905096803988971048)
XLA Ops:
  0.6 0.0 copy-start.8
  0.6 0.0 copy-start.9
  0.7 0.0 copy-start.6
  0.7 0.0 copy-start.7
  0.7 0.0 copy-start.4
  0.7 0.0 copy-start.5
  0.7 0.0 copy-start.3
  0.7 0.6 %copy-done.8 = f32[256]{0:T(256)S(1)} copy-done((f32[256]{0:T(256)S(1)}, f32[256]{0:T(256)}, u32[]{:S(2)}) %copy-start.8) | copy-done | bytes 1048
  1.3 0.0 copy-done.9
  1.3 0.0 copy-done.6
  1.3 0.0 copy-done.7
  1.4 0.0 copy-done.4
  1.4 0.0 copy-done.5
  1.4 0.0 copy-done.3
  1.4 0.0 copy-start
  1.4 0.9 %copy-done = f32[3,8,16,128]{3,2,1,0:T(8,128)S(1)} copy-done((f32[3,8,16,128]{3,2,1,0:T(8,128)S(1)}, f32[3,8,16,128]{3,2,1,0:T(8,128)}, u32[]{:S(2)}) %copy-start) | copy-done | bytes 196632
  2.3 0.0 copy-start.1
  2.3 0.9 %copy-done.1 = f32[3,8,16,128]{3,2,1,0:T(8,128)S(1)} copy-done((f32[3,8,16,128]{3,2,1,0:T(8,128)S(1)}, f32[3,8,16,128]{3,2,1,0:T(8,128)}, u32[]{:S(2)}) %copy-start.1) | copy-done | bytes 196632
  3.3 0.0 copy-start.2
  3.3 0.8 %copy-done.2 = f32[8,16,128]{2,1,0:T(8,128)S(1)} copy-done((f32[8,16,128]{2,1,0:T(8,128)S(1)}, f32[8,16,128]{2,1,0:T(8,128)}, u32[]{:S(2)}) %copy-start.2) | copy-done | bytes 65560
  4.1 44.7 %shard_map.121 = (f32[3,8,16,128]{3,2,1,0:T(8,128)S(1)}, f32[3,8,16,128]{3,2,1,0:T(8,128)S(1)}, f32[1,256]{1,0:T(1,128)S(1)}) custom-call(f32[3,8,16,128]{3,2,1,0:T(8,128)S(1)} %copy-done, f32[3,8,16,128]{3,2,1,0:T(8,128)S(1)} %copy-done.1, f32[8,16,128]{2,1,0:T(8,128)S(1)} %copy-done.2, s32[1,256]{1,0:T(1,128)S(1)} %bitcast.8, s32[1,256]{1,0:T(1,128)S(1)} %bitcast.9, ...), custom_call_target="tpu_custom_call" | custom-call | tf_op jit(solution)/shard_map/pallas_call | solution.py:542
  48.8 0.7 %copy.16 = f32[3,8,16,128]{3,2,1,0:T(8,128)} copy(f32[3,8,16,128]{3,2,1,0:T(8,128)S(1)} %get-tuple-element.12) | data formatting | bytes 393216
  49.5 0.7 %copy.17 = f32[3,8,16,128]{3,2,1,0:T(8,128)} copy(f32[3,8,16,128]{3,2,1,0:T(8,128)S(1)} %get-tuple-element.13) | data formatting | bytes 393216
  50.2 0.6 %copy.18 = f32[256]{0:T(256)} copy(f32[256]{0:T(256)S(1)} %bitcast.15) | data formatting | bytes 2048
Async XLA Ops:
  0.6 0.7 %copy-start.8 = (f32[256]{0:T(256)S(1)}, f32[256]{0:T(256)}, u32[]{:S(2)}) copy-start(f32[256]{0:T(256)} %param.18) | copy-start | bytes 3076
  0.6 0.7 %copy-start.9 = (f32[256]{0:T(256)S(1)}, f32[256]{0:T(256)}, u32[]{:S(2)}) copy-start(f32[256]{0:T(256)} %param.19) | copy-start | bytes 3076
  0.7 0.7 %copy-start.6 = (f32[256]{0:T(256)S(1)}, f32[256]{0:T(256)}, u32[]{:S(2)}) copy-start(f32[256]{0:T(256)} %param.16) | copy-start | bytes 3076
  0.7 0.7 %copy-start.7 = (f32[256]{0:T(256)S(1)}, f32[256]{0:T(256)}, u32[]{:S(2)}) copy-start(f32[256]{0:T(256)} %param.17) | copy-start | bytes 3076
  0.7 0.7 %copy-start.4 = (s32[256,1]{0,1:T(1,128)S(1)}, s32[256,1]{0,1:T(1,128)}, u32[]{:S(2)}) copy-start(s32[256,1]{0,1:T(1,128)} %param.14) | copy-start | bytes 3076
  0.7 0.7 %copy-start.5 = (s32[256]{0:T(256)S(1)}, s32[256]{0:T(256)}, u32[]{:S(2)}) copy-start(s32[256]{0:T(256)} %param.15) | copy-start | bytes 3076
  0.7 0.7 %copy-start.3 = (s32[256]{0:T(256)S(1)}, s32[256]{0:T(256)}, u32[]{:S(2)}) copy-start(s32[256]{0:T(256)} %param.13) | copy-start | bytes 3076
  1.4 0.9 %copy-start = (f32[3,8,16,128]{3,2,1,0:T(8,128)S(1)}, f32[3,8,16,128]{3,2,1,0:T(8,128)}, u32[]{:S(2)}) copy-start(f32[3,8,16,128]{3,2,1,0:T(8,128)} %e_ref.1) | copy-start | bytes 589828
  2.3 0.9 %copy-start.1 = (f32[3,8,16,128]{3,2,1,0:T(8,128)S(1)}, f32[3,8,16,128]{3,2,1,0:T(8,128)}, u32[]{:S(2)}) copy-start(f32[3,8,16,128]{3,2,1,0:T(8,128)} %ep_ref.1) | copy-start | bytes 589828
  3.3 0.8 %copy-start.2 = (f32[8,16,128]{2,1,0:T(8,128)S(1)}, f32[8,16,128]{2,1,0:T(8,128)}, u32[]{:S(2)}) copy-start(f32[8,16,128]{2,1,0:T(8,128)} %co_ref.1) | copy-start | bytes 196612

commit v2 on v1

v2 whole, which is shorter than its diff:
```python
import jax
import jax.numpy as jnp
from jax import lax
from jax.experimental import pallas as pl
from jax.experimental.pallas import tpu as pltpu
from jax.sharding import PartitionSpec as P

MESH = pl.DeviceIdType.MESH
F32 = jnp.float32
BF16 = jnp.bfloat16
N = 8
W = 4
CX, CY, CZ = 8, 16, 128
EX, EY = CX + 2 * W, CY + 2 * W
PORTS = 256
GROUPS = 8
NPAR = 5


def pieces(value):
    high = value.astype(BF16).astype(F32)
    rest = value - high
    mid = rest.astype(BF16).astype(F32)
    return high, mid, rest - mid


def dot_nt(a, b):
    return lax.dot_general(a, b, (((1,), (1,)), ((), ())), preferred_element_type=F32)


def dot_nn(a, b):
    return lax.dot_general(a, b, (((1,), (0,)), ((), ())), preferred_element_type=F32)


def three(dot, value, other):
    rows = value.shape[0]
    out = dot(jnp.concatenate(pieces(value), axis=0).astype(BF16), other)
    return (out[:rows] + out[rows : 2 * rows]) + out[2 * rows :]


def run(name, phase):
    phase()


def up_z(main, halo, lane):
    rm, rh = pltpu.roll(main, CZ - 1, 1), pltpu.roll(halo, CZ - 1, 1)
    return jnp.where(lane == CZ - 1, rh, rm), jnp.where(lane == CZ - 1, rm, rh)


def down_z(main, halo, lane):
    rm, rh = pltpu.roll(main, 1, 1), pltpu.roll(halo, 1, 1)
    return jnp.where(lane == 0, rh, rm), jnp.where(lane == 0, rm, rh)


def up_y(v):
    return pltpu.roll(v, EY - 1, 0)


def down_y(v):
    return pltpu.roll(v, 1, 0)


def substep(now, now_h, old, old_h, cou, cou_h, low, high, last):
    lane = lax.broadcasted_iota(jnp.int32, (EY, CZ), 1)

    def curls(x):
        vx, vy, vz = now[0, x], now[1, x], now[2, x]
        vxh, vyh, vzh = now_h[0, x], now_h[1, x], now_h[2, x]
        vxu, vxuh = up_z(vx, vxh, lane)
        gy = (vxu - vx) - (now[2, x + 1] - vz)
        gyh = (vxuh - vxh) - (now_h[2, x + 1] - vzh)
        gz = (now[1, x + 1] - vy) - (up_y(vx) - vx)
        gzh = (now_h[1, x + 1] - vyh) - (up_y(vxh) - vxh)
        return gy, gyh, gz, gzh

    def body(x, carry):
        gyp, gyph, gzp, gzph = carry
        vx, vy, vz = now[0, x], now[1, x], now[2, x]
        vxh, vyh, vzh = now_h[0, x], now_h[1, x], now_h[2, x]
        gy, gyh, gz, gzh = curls(x)
        vyu, vyuh = up_z(vy, vyh, lane)
        gx = (up_y(vz) - vz) - (vyu - vy)
        gxh = (up_y(vzh) - vzh) - (vyuh - vyh)
        gxd, gxdh = down_z(gx, gxh, lane)
        gyd, gydh = down_z(gy, gyh, lane)
        c = cou[x]
        kx = (gz - down_y(gz)) - (gy - gyd)
        ky = (gx - gxd) - (gz - gzp)
        kz = (gy - gyp) - (gx - down_y(gx))
        old[0, x] = 2.0 * vx - old[0, x] - c * kx
        old[1, x] = 2.0 * vy - old[1, x] - c * ky
        old[2, x] = 2.0 * vz - old[2, x] - c * kz
        if not last:
            ch = cou_h[x]
            kxh = (gzh - down_y(gzh)) - (gyh - gydh)
            kyh = (gxh - gxdh) - (gzh - gzph)
            kzh = (gyh - gyph) - (gxh - down_y(gxh))
            old_h[0, x] = 2.0 * vxh - old_h[0, x] - ch * kxh
            old_h[1, x] = 2.0 * vyh - old_h[1, x] - ch * kyh
            old_h[2, x] = 2.0 * vzh - old_h[2, x] - ch * kzh
        return gy, gyh, gz, gzh

    carry = curls(low - 1)
    for x in range(low, high):
        carry = body(x, carry)


def kernel(
    e_ref,
    ep_ref,
    co_ref,
    cell_ref,
    route_ref,
    group_ref,
    gain_ref,
    drive_ref,
    bias_ref,
    couple_ref,
    next_ref,
    last_ref,
    cur_ref,
    own,
    a,
    ah,
    b,
    bh,
    c,
    ch,
    pz,
    px,
    py,
    pc,
    qz,
    qx,
    qy,
    qc,
    iport,
    fport,
    ownpar,
    ownsam,
    par,
    sam,
    node,
    drain,
    rowm,
    lanem,
    cellm,
    zm,
    sample8,
    current8,
    lsem,
    hsend,
    hrecv,
    ysend,
    yrecv,
    xsend,
    xrecv,
    tsem,
    ssend,
    srecv,
    plane,
):
    gx, gy, gz = lax.axis_index("gx"), lax.axis_index("gy"), lax.axis_index("gz")
    me = gz * N + gy

    def near(dx, dy, dz):
        return (lax.rem(gx + N + dx, N), lax.rem(gy + N + dy, N), lax.rem(gz + N + dz, N))

    barrier = pltpu.get_barrier_semaphore()

    greeted = [near(dx, dy, dz) for dx in (-1, 1) for dy in (-1, 0, 1) for dz in (-1, 0, 1)]
    greeted += [near(0, dy, dz) for dy in (-1, 1) for dz in (-1, 1)]
    greeted += [near(0, k, 0) for k in range(1, N)] + [near(0, 0, k) for k in range(1, N)]
    for device in greeted:
        pl.semaphore_signal(barrier, inc=1, device_id=device, device_id_type=MESH)

    inner = (pl.ds(W, CX), pl.ds(W, CY))
    local = [
        (e_ref, own.at[0:3]),
        (ep_ref, own.at[3:6]),
        (co_ref, own.at[6]),
        (cell_ref, iport.at[0]),
        (route_ref, iport.at[1]),
        (group_ref, iport.at[2]),
        (gain_ref, fport.at[0]),
        (drive_ref, fport.at[1]),
        (bias_ref, fport.at[2]),
        (couple_ref, fport.at[3]),
        (e_ref, a.at[:, inner[0], inner[1]]),
        (ep_ref, b.at[:, inner[0], inner[1]]),
        (co_ref, c.at[inner[0], inner[1]]),
    ]
    local = [pltpu.make_async_copy(s, d, lsem.at[i]) for i, (s, d) in enumerate(local)]
    for copy in local:
        copy.start()
    for copy in local[:3]:
        copy.wait()

    lane = lax.broadcasted_iota(jnp.int32, (CZ, CZ), 1)
    lane8 = lax.broadcasted_iota(jnp.int32, (8, CZ), 1)
    slot = lane8 % CY // W
    iota8 = lax.broadcasted_iota(jnp.int32, (8, PORTS), 0)

    def turn(v, shift):
        shift = shift % CZ
        return v if shift == 0 else pltpu.roll(v, shift, 1)

    def pack():
        packed = jnp.zeros((CZ, CZ), F32)
        for f in range(7):
            rolled = pltpu.roll(own[f].reshape(CZ, CZ), W + 8 * f, 1)
            packed = jnp.where(lane // 8 == f, rolled, packed)
        packed = packed.T
        rows = [packed[8 * f : 8 * f + 8] for f in range(7)]
        for f in range(7):
            pz[f] = rows[f]

        def quarters(group, top):
            out = turn(group[0], -12 if top else 0)
            for j in range(1, len(group)):
                out = jnp.where(slot == j, turn(group[j], 4 * j - (12 if top else 0)), out)
            return out

        halves = []
        for top in (0, 1):
            tiles = []
            for j in range(4):
                if j == 3:
                    tile = turn(rows[3], 64 * top)
                elif top:
                    tile = jnp.where(lane8 < 64, turn(rows[j], 64), rows[j + 4])
                else:
                    tile = jnp.where(lane8 < 64, rows[j], turn(rows[j + 4], 64))
                px[top, j] = tile
                tiles.append(tile)
            halves.append(tiles)
        for top in (0, 1):
            py[top, 0] = quarters(rows[0:4], top)
            py[top, 1] = quarters(rows[4:7], top)
            for xt in (0, 1):
                pc[xt, top] = quarters(halves[xt], top)

    run("pack", pack)

    for copy in local[3:]:
        copy.wait()
    def ports():
        route = iport[1]
        at64 = lax.broadcasted_iota(jnp.int32, (64, PORTS), 0) == route
        earlier = lax.broadcasted_iota(jnp.int32, (PORTS, PORTS), 0) < lax.broadcasted_iota(
            jnp.int32, (PORTS, PORTS), 1
        )
        count = dot_nn(
            jnp.where(at64, 1.0, 0.0).astype(BF16), jnp.where(earlier, 1.0, 0.0).astype(BF16)
        )
        rank = jnp.sum(jnp.where(at64, count, 0.0), axis=0, keepdims=True).astype(jnp.int32)
        slot_lane = route + 64 * (rank % 2)
        slot_row = rank // 2
        iota128 = lax.broadcasted_iota(jnp.int32, (CZ, PORTS), 0)
        lanem[...] = jnp.where(iota128 == slot_lane, 1.0, 0.0).astype(BF16)
        in_row = iota8 % 4 == slot_row
        rowm[...] = jnp.where(in_row, 1.0, 0.0)
        values = [fport[0], fport[1], fport[2], fport[3], iport[2].astype(F32) + 1.0]
        stacked = jnp.concatenate(
            [
                jnp.where(in_row, jnp.where(iota8 < 4, values[2 * i], values[min(2 * i + 1, 4)]), 0.0)
                for i in range(3)
            ],
            axis=0,
        )
        slots = three(dot_nt, stacked, lanem[...])
        for i in range(NPAR):
            ownpar[i] = slots[4 * i : 4 * i + 4]
        cell = iport[0]
        cellm[...] = jnp.where(iota128 == cell // CZ, 1.0, 0.0).astype(BF16)
        zm[...] = jnp.where(iota128 == cell % CZ, 1.0, 0.0).astype(BF16)

    run("ports", ports)

    pl.semaphore_wait(barrier, len(greeted))
    for k in range(1, N):
        pl.semaphore_signal(plane, inc=1, device_id=near(0, k, 0), device_id_type=MESH)

    def span(d, width, size):
        if d == 0:
            return pl.ds(0, size), pl.ds(W, size)
        if d > 0:
            return pl.ds(size - width, width), pl.ds(W - width, width)
        return pl.ds(0, width), pl.ds(W + size, width)

    halo = []

    def send(src, dst, d):
        i = len(halo)
        copy = pltpu.make_async_remote_copy(
            src_ref=src,
            dst_ref=dst,
            send_sem=hsend.at[i],
            recv_sem=hrecv.at[i],
            device_id=near(*d),
            device_id_type=MESH,
        )
        copy.start()
        halo.append(copy)

    for dz in (1, -1):
        part = pl.ds(0, W) if dz > 0 else pl.ds(W, W)
        send(pz.at[:, part], qz.at[:, part], (0, 0, dz))
        for d in (1, -1):
            mine, theirs = (1, 0) if d > 0 else (0, 1)
            send(px.at[mine, :, part], qx.at[theirs, :, part], (d, 0, dz))
            send(py.at[mine, :, part], qy.at[theirs, :, part], (0, d, dz))
            for dy in (1, -1):
                mine_y, theirs_y = (1, 0) if dy > 0 else (0, 1)
                send(pc.at[mine, mine_y, part], qc.at[theirs, theirs_y, part], (d, dy, dz))
    n_z = len(halo)
    flat = [(0, 1), (0, -1), (1, 0), (-1, 0), (1, 1), (1, -1), (-1, 1), (-1, -1)]
    for dx, dy in flat:
        sx4, tx4 = span(dx, W, CX)
        sy4, ty4 = span(dy, W, CY)
        sx3, tx3 = span(dx, W - 1, CX)
        sy3, ty3 = span(dy, W - 1, CY)
        send(own.at[0:3, sx4, sy4], a.at[:, tx4, ty4], (dx, dy, 0))
        send(own.at[3:6, sx3, sy3], b.at[:, tx3, ty3], (dx, dy, 0))
        send(own.at[6, sx3, sy3], c.at[tx3, ty3], (dx, dy, 0))

    half = pl.ds(4 * lax.rem(gy, 2), 4)
    spread_y = []
    for k in range(1, N):
        copy = pltpu.make_async_remote_copy(
            src_ref=ownpar,
            dst_ref=par.at[gz, gy // 2, :, half],
            send_sem=ysend.at[k - 1],
            recv_sem=yrecv.at[k - 1],
            device_id=(gx, lax.rem(gy + k, N), gz),
            device_id_type=MESH,
        )
        copy.start()
        spread_y.append(copy)
    own_par = pltpu.make_async_copy(ownpar, par.at[gz, gy // 2, :, half], lsem.at[0])
    own_par.start()

    for copy in halo[:n_z]:
        copy.wait_recv()
    low_ok = jnp.where(gz > 0, 1, 0)
    high_ok = jnp.where(gz < N - 1, 1, 0)
    keep = jnp.where(lane < CZ // 2, high_ok, low_ok) == 1

    def unpack(tiles, store):
        block = jnp.concatenate(tiles + [jnp.zeros((CZ - 56, CZ), F32)], axis=0).T
        for f in range(7):
            value = jnp.where(keep, pltpu.roll(block, (CZ - 8 * f - W) % CZ, 1), 0.0)
            ref = (ah, bh, ch)[f // 3]
            store(ref if f == 6 else ref.at[f % 3], value)

    def store_own(ref, value):
        ref[W : W + CX, W : W + CY] = value.reshape(CX, CY, CZ)

    def store_x(ref, value):
        value = value.reshape(CX, CY, CZ)
        ref[0:W, W : W + CY] = value[:W]
        ref[W + CX :, W : W + CY] = value[W:]

    def store_y(ref, value):
        value = value.reshape(CX, 4, W, CZ)
        ref[W : W + CX, 0:W] = value[:, 0]
        ref[W : W + CX, W + CY :] = value[:, 1]
        ref[0:W, 0:W] = value[:W, 2]
        ref[W + CX :, 0:W] = value[W:, 2]
        ref[0:W, W + CY :] = value[:W, 3]
        ref[W + CX :, W + CY :] = value[W:, 3]

    def unpack_all():
        unpack([qz[f] for f in range(7)], store_own)
        tiles = []
        for f in range(7):
            h, j = f // 4, f % 4
            if h == 0:
                tiles.append(jnp.where(lane8 < 64, qx[0, j], pltpu.roll(qx[1, j], 64, 1)))
            else:
                tiles.append(jnp.where(lane8 < 64, pltpu.roll(qx[0, j], 64, 1), qx[1, j]))
        unpack(tiles, store_x)
        tiles = []
        for f in range(7):
            h, j = f // 4, f % 4
            tile = jnp.where(slot == 0, turn(qy[0, h], -4 * j), turn(qy[1, h], 4 - 4 * j))
            for s in (0, 1):
                shift = 8 + 4 * s - 4 * j - 64 * h
                corner = jnp.where(lane8 < 64, turn(qc[0, s], shift), turn(qc[1, s], shift + 64))
                tile = jnp.where(slot == 2 + s, corner, tile)
            tiles.append(tile)
        unpack(tiles, store_y)

    run("unpack", unpack_all)

    def clear(xs, ys):
        for ref in (a, ah, b, bh):
            ref[:, xs, ys] = jnp.zeros_like(ref[:, xs, ys])
        for ref in (c, ch):
            ref[xs, ys] = jnp.zeros_like(ref[xs, ys])

    def clear_y(parts):
        @pl.when(gy == 0)
        def _():
            for xs in parts:
                clear(xs, slice(0, W))

        @pl.when(gy == N - 1)
        def _():
            for xs in parts:
                clear(xs, slice(W + CY, EY))

    for copy in halo[n_z : n_z + 6]:
        copy.wait_recv()
    clear_y([slice(W, W + CX)])

    def early():
        substep(a, ah, b, bh, c, ch, 5, 11, False)
        substep(b, bh, a, ah, c, ch, 6, 10, False)
        substep(a, ah, b, bh, c, ch, 7, 9, False)

    run("early", early)

    own_par.wait()
    for copy in spread_y:
        copy.wait_recv()
    spread_x = []
    for k in range(1, 4):
        copy = pltpu.make_async_remote_copy(
            src_ref=par.at[gz],
            dst_ref=par.at[gz],
            send_sem=xsend.at[k - 1],
            recv_sem=xrecv.at[k - 1],
            device_id=(gx, gy, lax.rem(gz + 2 * k, N)),
            device_id_type=MESH,
        )
        copy.start()
        spread_x.append(copy)

    for copy in halo[n_z + 6 :]:
        copy.wait_recv()
    clear_y([slice(0, W), slice(W + CX, EX)])

    @pl.when(gx == 0)
    def _():
        clear(slice(0, W), slice(0, EY))

    @pl.when(gx == N - 1)
    def _():
        clear(slice(W + CX, EX), slice(0, EY))

    def late():
        substep(a, ah, b, bh, c, ch, 1, 5, False)
        substep(a, ah, b, bh, c, ch, 11, 15, False)
        substep(b, bh, a, ah, c, ch, 2, 6, False)
        substep(b, bh, a, ah, c, ch, 10, 14, False)
        substep(a, ah, b, bh, c, ch, 3, 7, False)
        substep(a, ah, b, bh, c, ch, 9, 13, False)

    run("late", late)
    out_last = pltpu.make_async_copy(b.at[:, inner[0], inner[1]], last_ref, lsem.at[1])
    out_last.start()
    run("step4", lambda: substep(b, bh, a, ah, c, ch, 4, EX - 4, True))
    out_next = pltpu.make_async_copy(
        a.at[0:2, inner[0], inner[1]], next_ref.at[0:2], lsem.at[2]
    )
    out_next.start()

    def take():
        ez = a[2, W : W + CX, W : W + CY].reshape(CZ, CZ)
        picked = three(dot_nn, ez.T, cellm[...])
        sample = jnp.sum(picked * zm[...].astype(F32), axis=0, keepdims=True)
        found = three(dot_nt, rowm[...] * sample, lanem[...])
        sample8[...] = found
        ownsam[...] = found[0:4]

    run("take", take)
    pl.semaphore_wait(plane, N - 1)
    for k in range(1, N * N):
        t = lax.rem(me + k, N * N)
        pltpu.make_async_remote_copy(
            src_ref=ownsam,
            dst_ref=sam.at[gz, gy // 2, half],
            send_sem=ssend,
            recv_sem=srecv,
            device_id=(gx, lax.rem(t, N), t // N),
            device_id_type=MESH,
        ).start()
    own_sam = pltpu.make_async_copy(ownsam, sam.at[gz, gy // 2, half], lsem.at[0])
    own_sam.start()

    for copy in spread_x:
        copy.wait_recv()
    core = lax.rem(gz, 2)
    twins = []
    for i in range(4):
        copy = pltpu.make_async_remote_copy(
            src_ref=par.at[2 * i + core],
            dst_ref=par.at[2 * i + core],
            send_sem=tsem.at[0, i],
            recv_sem=tsem.at[1, i],
            device_id=(gx, gy, gz + 1 - 2 * core),
            device_id_type=MESH,
        )
        copy.start()
        twins.append(copy)
    for copy in twins:
        copy.wait_recv()
    own_sam.wait()
    pltpu.make_async_copy(drain, drain, srecv).wait()

    def solve():
        sub = lax.broadcasted_iota(jnp.int32, (8, CZ), 0)

        def totals(first):
            def add(i, acc):
                for j in range(N // 2):
                    volt = sam[i, j] if first else node[i, j]
                    s = jnp.tanh(volt)
                    grp = par[i, j, 4]
                    acc = tuple(
                        acc[g] + jnp.where(grp == float(g + 1), s, 0.0) for g in range(GROUPS)
                    )
                return acc

            acc = lax.fori_loop(0, N, add, tuple(jnp.zeros((8, CZ), F32) for _ in range(GROUPS)))
            total = jnp.zeros((8, CZ), F32)
            for g in range(GROUPS):
                total = jnp.where(sub == g, jnp.sum(acc[g], axis=0, keepdims=True), total)
            return total + pltpu.roll(total, 64, 1)

        def newton(volt, sample, gain, drive, bias, couple, grp, total):
            s = jnp.tanh(volt)
            shared = jnp.zeros_like(volt)
            for g in range(GROUPS):
                shared = jnp.where(grp == float(g + 1), total[g : g + 1], shared)
            resid = (1.0 + gain) * volt - sample - bias + drive * s + couple * shared
            slope = 1.0 + gain + (drive + couple) * (1.0 - s * s)
            return volt - resid / slope

        mine = sample8[...]
        my = [ownpar[i] for i in range(NPAR)]
        my = [jnp.concatenate([v, v], axis=0) for v in my]
        volt = mine
        for iterate in range(3):
            total = totals(iterate == 0)
            volt = newton(volt, mine, *my, total)
            if iterate < 2:

                def move(i, _):
                    for j in range(N // 2):
                        start = sam[i, j]
                        now = start if iterate == 0 else node[i, j]
                        node[i, j] = newton(
                            now, start, *[par[i, j, p] for p in range(NPAR)], total
                        )
                    return 0

                lax.fori_loop(0, N, move, 0)
        current8[...] = my[0] * (volt - mine)

    run("solve", solve)

    def back():
        spread = three(dot_nn, current8[...], lanem[...])
        port = jnp.sum(jnp.where(iota8 < 4, rowm[...] * spread, 0.0), axis=0, keepdims=True)
        cur_ref[...] = port
        extra = three(dot_nt, cellm[...].astype(F32) * port, zm[...])
        next_ref[2] = (a[2, W : W + CX, W : W + CY].reshape(CZ, CZ) + extra).reshape(CX, CY, CZ)

    run("back", back)
    for copy in (out_last, out_next):
        copy.wait()
    for copy in halo + spread_y + spread_x + twins:
        copy.wait_send()
    pltpu.make_async_copy(drain, drain, ssend).wait()


def on_device(e, ep, co, cell, route, group, gain, drive, bias, couple):
    line = lambda v: v.reshape(1, PORTS)
    any_spec = pl.BlockSpec(memory_space=pl.ANY)
    dma = pltpu.SemaphoreType.DMA
    ext, ext1 = pltpu.VMEM((3, EX, EY, CZ), F32), pltpu.VMEM((EX, EY, CZ), F32)
    electric, last, current = pl.pallas_call(
        kernel,
        out_shape=(
            pltpu.VMEM((3, CX, CY, CZ), F32),
            pltpu.VMEM((3, CX, CY, CZ), F32),
            pltpu.VMEM((1, PORTS), F32),
        ),
        in_specs=[any_spec] * 10,
        out_specs=(pl.BlockSpec(memory_space=pltpu.VMEM),) * 3,
        scratch_shapes=[
            pltpu.VMEM((7, CX, CY, CZ), F32),
            ext,
            ext,
            ext,
            ext,
            ext1,
            ext1,
            pltpu.VMEM((7, 8, CZ), F32),
            pltpu.VMEM((2, 4, 8, CZ), F32),
            pltpu.VMEM((2, 2, 8, CZ), F32),
            pltpu.VMEM((2, 2, 8, CZ), F32),
            pltpu.VMEM((7, 8, CZ), F32),
            pltpu.VMEM((2, 4, 8, CZ), F32),
            pltpu.VMEM((2, 2, 8, CZ), F32),
            pltpu.VMEM((2, 2, 8, CZ), F32),
            pltpu.VMEM((3, 1, PORTS), jnp.int32),
            pltpu.VMEM((4, 1, PORTS), F32),
            pltpu.VMEM((NPAR, 4, CZ), F32),
            pltpu.VMEM((4, CZ), F32),
            pltpu.VMEM((N, N // 2, NPAR, 8, CZ), F32),
            pltpu.VMEM((N, N // 2, 8, CZ), F32),
            pltpu.VMEM((N, N // 2, 8, CZ), F32),
            pltpu.VMEM((N * N - 1, 4, CZ), F32),
            pltpu.VMEM((8, PORTS), F32),
            pltpu.VMEM((CZ, PORTS), BF16),
            pltpu.VMEM((CZ, PORTS), BF16),
            pltpu.VMEM((CZ, PORTS), BF16),
            pltpu.VMEM((8, CZ), F32),
            pltpu.VMEM((8, CZ), F32),
            dma((13,)),
            dma((42,)),
            dma((42,)),
            dma((N - 1,)),
            dma((N - 1,)),
            dma((3,)),
            dma((3,)),
            dma((2, 4)),
            dma,
            dma,
            pltpu.SemaphoreType.REGULAR,
        ],
        compiler_params=pltpu.CompilerParams(
            collective_id=0, has_side_effects=True, vmem_limit_bytes=56 * 1024 * 1024
        ),
    )(e, ep, co, line(cell), line(route), line(group), line(gain), line(drive), line(bias), line(couple))
    return electric, last, current.reshape(PORTS)


def solution(mesh):
    field = P(None, "gx", "gy", "gz")
    port = P(("gx", "gy", "gz"))
    placed = (
        field,
        field,
        P("gx", "gy", "gz"),
        port,
        P(("gx", "gy", "gz"), None),
        port,
        port,
        port,
        port,
        port,
    )
    return jax.shard_map(
        on_device,
        mesh=mesh,
        in_specs=placed,
        out_specs=(field, field, port),
        check_vma=False,
    )
```

time: 51 us -> 40.8 us (0.80)
  Pallas kernels: 44.7 us -> 38.1 us
  local copies, waits for them, and re-layouts: 5.33 us -> 1.92 us
    pallas_call x1, Pallas kernels: 44.7 us -> 38.1 us  [on_device(): pl.pallas_call(kernel, out_shape=(pltpu.VMEM((3, CX, CY, CZ), F32), pltpu...]
    unnamed x23 -> x3, local copies, waits for them, and re-layouts: 5.33 us -> 1.92 us
where the time goes in v2:
time: 40.8 us; the launch traced here: 40.6 us
  Pallas kernels  38.1 us (93%)
  local copies, waits for them, and re-layouts  1.92 us (5%)
  between operations  0.64 us (2%)
    pallas_call x1, Pallas kernels, on_device(): pl.pallas_call(kernel, out_shape=(pltpu.VMEM((3, CX, CY, CZ), F32), pltpu...  38.1 us
    unnamed x3, local copies, waits for them, and re-layouts  1.92 us

profile of v2, /device:TPU:1, one launch (start us, length us, event | category | flops | bytes accessed | tf_op | source)
XLA Modules:
  0.0 40.6 jit_solution(12673634454955652634)
XLA Ops:
  0.6 38.1 %shard_map.121 = (f32[3,8,16,128]{3,2,1,0:T(8,128)S(1)}, f32[3,8,16,128]{3,2,1,0:T(8,128)S(1)}, f32[1,256]{1,0:T(1,128)S(1)}) custom-call(f32[3,8,16,128]{3,2,1,0:T(8,128)} %e_ref.1, f32[3,8,16,128]{3,2,1,0:T(8,128)} %ep_ref.1, f32[8,16,128]{2,1,0:T(8,128)} %co_ref.1, s32[1,256]{1,0:T(1,128)} %bitcast.9, s32[1,256]{1,0:T(1,128)} %bitcast.10, ...), custom_call_target="tpu_custom_call" | custom-call | tf_op jit(solution)/shard_map/pallas_call | solution.py:584
  38.7 0.7 %copy.16 = f32[3,8,16,128]{3,2,1,0:T(8,128)} copy(f32[3,8,16,128]{3,2,1,0:T(8,128)S(1)} %get-tuple-element.9) | data formatting | bytes 393216
  39.4 0.6 %copy.18 = f32[256]{0:T(256)} copy(f32[256]{0:T(256)S(1)} %bitcast.8) | data formatting | bytes 2048
  40.0 0.7 %copy.17 = f32[3,8,16,128]{3,2,1,0:T(8,128)} copy(f32[3,8,16,128]{3,2,1,0:T(8,128)S(1)} %get-tuple-element.10) | data formatting | bytes 393216

commit v3 on v2

--- a/solution.py
+++ b/solution.py
@@ -64,40 +64,40 @@
     lane = lax.broadcasted_iota(jnp.int32, (EY, CZ), 1)
 
     def curls(x):
-        vx, vy, vz = now[0, x], now[1, x], now[2, x]
-        vxh, vyh, vzh = now_h[0, x], now_h[1, x], now_h[2, x]
+        vx, vy, vz = now[0, x, 0:EY], now[1, x, 0:EY], now[2, x, 0:EY]
+        vxh, vyh, vzh = now_h[0, x, 0:EY], now_h[1, x, 0:EY], now_h[2, x, 0:EY]
         vxu, vxuh = up_z(vx, vxh, lane)
-        gy = (vxu - vx) - (now[2, x + 1] - vz)
-        gyh = (vxuh - vxh) - (now_h[2, x + 1] - vzh)
-        gz = (now[1, x + 1] - vy) - (up_y(vx) - vx)
-        gzh = (now_h[1, x + 1] - vyh) - (up_y(vxh) - vxh)
+        gy = (vxu - vx) - (now[2, x + 1, 0:EY] - vz)
+        gyh = (vxuh - vxh) - (now_h[2, x + 1, 0:EY] - vzh)
+        gz = (now[1, x + 1, 0:EY] - vy) - (now[0, x, 1 : EY + 1] - vx)
+        gzh = (now_h[1, x + 1, 0:EY] - vyh) - (now_h[0, x, 1 : EY + 1] - vxh)
         return gy, gyh, gz, gzh
 
     def body(x, carry):
         gyp, gyph, gzp, gzph = carry
-        vx, vy, vz = now[0, x], now[1, x], now[2, x]
-        vxh, vyh, vzh = now_h[0, x], now_h[1, x], now_h[2, x]
+        vx, vy, vz = now[0, x, 0:EY], now[1, x, 0:EY], now[2, x, 0:EY]
+        vxh, vyh, vzh = now_h[0, x, 0:EY], now_h[1, x, 0:EY], now_h[2, x, 0:EY]
         gy, gyh, gz, gzh = curls(x)
         vyu, vyuh = up_z(vy, vyh, lane)
-        gx = (up_y(vz) - vz) - (vyu - vy)
-        gxh = (up_y(vzh) - vzh) - (vyuh - vyh)
+        gx = (now[2, x, 1 : EY + 1] - vz) - (vyu - vy)
+        gxh = (now_h[2, x, 1 : EY + 1] - vzh) - (vyuh - vyh)
         gxd, gxdh = down_z(gx, gxh, lane)
         gyd, gydh = down_z(gy, gyh, lane)
-        c = cou[x]
+        c = cou[x, 0:EY]
         kx = (gz - down_y(gz)) - (gy - gyd)
         ky = (gx - gxd) - (gz - gzp)
         kz = (gy - gyp) - (gx - down_y(gx))
-        old[0, x] = 2.0 * vx - old[0, x] - c * kx
-        old[1, x] = 2.0 * vy - old[1, x] - c * ky
-        old[2, x] = 2.0 * vz - old[2, x] - c * kz
+        old[0, x, 0:EY] = 2.0 * vx - old[0, x, 0:EY] - c * kx
+        old[1, x, 0:EY] = 2.0 * vy - old[1, x, 0:EY] - c * ky
+        old[2, x, 0:EY] = 2.0 * vz - old[2, x, 0:EY] - c * kz
         if not last:
-            ch = cou_h[x]
+            ch = cou_h[x, 0:EY]
             kxh = (gzh - down_y(gzh)) - (gyh - gydh)
             kyh = (gxh - gxdh) - (gzh - gzph)
             kzh = (gyh - gyph) - (gxh - down_y(gxh))
-            old_h[0, x] = 2.0 * vxh - old_h[0, x] - ch * kxh
-            old_h[1, x] = 2.0 * vyh - old_h[1, x] - ch * kyh
-            old_h[2, x] = 2.0 * vzh - old_h[2, x] - ch * kzh
+            old_h[0, x, 0:EY] = 2.0 * vxh - old_h[0, x, 0:EY] - ch * kxh
+            old_h[1, x, 0:EY] = 2.0 * vyh - old_h[1, x, 0:EY] - ch * kyh
+            old_h[2, x, 0:EY] = 2.0 * vzh - old_h[2, x, 0:EY] - ch * kzh
         return gy, gyh, gz, gzh
 
     carry = curls(low - 1)
@@ -161,18 +161,9 @@
     plane,
 ):
     gx, gy, gz = lax.axis_index("gx"), lax.axis_index("gy"), lax.axis_index("gz")
-    me = gz * N + gy
 
     def near(dx, dy, dz):
         return (lax.rem(gx + N + dx, N), lax.rem(gy + N + dy, N), lax.rem(gz + N + dz, N))
-
-    barrier = pltpu.get_barrier_semaphore()
-
-    greeted = [near(dx, dy, dz) for dx in (-1, 1) for dy in (-1, 0, 1) for dz in (-1, 0, 1)]
-    greeted += [near(0, dy, dz) for dy in (-1, 1) for dz in (-1, 1)]
-    greeted += [near(0, k, 0) for k in range(1, N)] + [near(0, 0, k) for k in range(1, N)]
-    for device in greeted:
-        pl.semaphore_signal(barrier, inc=1, device_id=device, device_id_type=MESH)
 
     inner = (pl.ds(W, CX), pl.ds(W, CY))
     local = [
@@ -191,7 +182,32 @@
         (co_ref, c.at[inner[0], inner[1]]),
     ]
     local = [pltpu.make_async_copy(s, d, lsem.at[i]) for i, (s, d) in enumerate(local)]
-    for copy in local:
+    for copy in local[:3]:
+        copy.start()
+
+    barrier = pltpu.get_barrier_semaphore()
+
+    greeted = [near(0, dy, dz) for dy in (-1, 1) for dz in (-1, 1)]
+    greeted += [near(0, k, 0) for k in range(1, N)] + [near(0, 0, k) for k in range(1, N)]
+
+    def has(d):
+        return gx < N - 1 if d > 0 else gx > 0
+
+    def greet(device):
+        pl.semaphore_signal(barrier, inc=1, device_id=device, device_id_type=MESH)
+
+    for dx in (-1, 1):
+
+        @pl.when(has(dx))
+        def _():
+            for dy in (-1, 0, 1):
+                for dz in (-1, 0, 1):
+                    greet(near(dx, dy, dz))
+
+    for device in greeted:
+        greet(device)
+
+    for copy in local[3:]:
         copy.start()
     for copy in local[:3]:
         copy.wait()
@@ -241,6 +257,74 @@
                 pc[xt, top] = quarters(halves[xt], top)
 
     run("pack", pack)
+
+    beside = jnp.where(gx > 0, 9, 0) + jnp.where(gx < N - 1, 9, 0)
+    pl.semaphore_wait(barrier, len(greeted) + beside)
+    for k in range(1, N):
+        pl.semaphore_signal(plane, inc=1, device_id=near(0, k, 0), device_id_type=MESH)
+
+    def span(d, width, size):
+        if d == 0:
+            return pl.ds(0, size), pl.ds(W, size)
+        if d > 0:
+            return pl.ds(size - width, width), pl.ds(W - width, width)
+        return pl.ds(0, width), pl.ds(W + size, width)
+
+    halo = []
+
+    def send(src, dst, d):
+        i = len(halo)
+        copy = pltpu.make_async_remote_copy(
+            src_ref=src,
+            dst_ref=dst,
+            send_sem=hsend.at[i],
+            recv_sem=hrecv.at[i],
+            device_id=near(*d),
+            device_id_type=MESH,
+        )
+        if d[0]:
+            pl.when(has(d[0]))(copy.start)
+        else:
+            copy.start()
+        halo.append((copy, d[0]))
+
+    def received(copies):
+        for copy, d in copies:
+            if d:
+                pl.when(has(-d))(copy.wait_recv)
+            else:
+                copy.wait_recv()
+
+    for dz in (1, -1):
+        part = pl.ds(0, W) if dz > 0 else pl.ds(W, W)
+        send(pz.at[:, part], qz.at[:, part], (0, 0, dz))
+        for d in (1, -1):
+            mine, theirs = (1, 0) if d > 0 else (0, 1)
+            send(px.at[mine, :, part], qx.at[theirs, :, part], (d, 0, dz))
+            send(py.at[mine, :, part], qy.at[theirs, :, part], (0, d, dz))
+            for dy in (1, -1):
+                mine_y, theirs_y = (1, 0) if dy > 0 else (0, 1)
+                send(pc.at[mine, mine_y, part], qc.at[theirs, theirs_y, part], (d, dy, dz))
+    n_z = len(halo)
+    flat = [(0, 1), (0, -1), (1, 0), (-1, 0), (1, 1), (1, -1), (-1, 1), (-1, -1)]
+    for dx, dy in flat:
+        sx4, tx4 = span(dx, W, CX)
+        sy4, ty4 = span(dy, W, CY)
+        sx3, tx3 = span(dx, W - 1, CX)
+        sy3, ty3 = span(dy, W - 1, CY)
+        if dx and dy:
+            for near_x, near_y in ((2, W), (W, 2)):
+                skip = 2 if near_x == W else 0
+                xs = pl.ds(CX - near_x, near_x - skip) if dx > 0 else pl.ds(skip, near_x - skip)
+                xt = pl.ds(W - near_x, near_x - skip) if dx > 0 else pl.ds(W + CX + skip, near_x - skip)
+                ys, yt = span(dy, near_y, CY)
+                send(own.at[0:3, xs, ys], a.at[:, xt, yt], (dx, dy, 0))
+            send(own.at[3:6, sx3, sy3], b.at[:, tx3, ty3], (dx, dy, 0))
+            send(own.at[6, sx3, sy3], c.at[tx3, ty3], (dx, dy, 0))
+            continue
+        send(own.at[0:3, sx4, sy4], a.at[:, tx4, ty4], (dx, dy, 0))
+        send(own.at[3:6, sx3, sy3], b.at[:, tx3, ty3], (dx, dy, 0))
+        send(own.at[6, sx3, sy3], c.at[tx3, ty3], (dx, dy, 0))
 
     for copy in local[3:]:
         copy.wait()
@@ -277,53 +361,6 @@
 
     run("ports", ports)
 
-    pl.semaphore_wait(barrier, len(greeted))
-    for k in range(1, N):
-        pl.semaphore_signal(plane, inc=1, device_id=near(0, k, 0), device_id_type=MESH)
-
-    def span(d, width, size):
-        if d == 0:
-            return pl.ds(0, size), pl.ds(W, size)
-        if d > 0:
-            return pl.ds(size - width, width), pl.ds(W - width, width)
-        return pl.ds(0, width), pl.ds(W + size, width)
-
-    halo = []
-
-    def send(src, dst, d):
-        i = len(halo)
-        copy = pltpu.make_async_remote_copy(
-            src_ref=src,
-            dst_ref=dst,
-            send_sem=hsend.at[i],
-            recv_sem=hrecv.at[i],
-            device_id=near(*d),
-            device_id_type=MESH,
-        )
-        copy.start()
-        halo.append(copy)
-
-    for dz in (1, -1):
-        part = pl.ds(0, W) if dz > 0 else pl.ds(W, W)
-        send(pz.at[:, part], qz.at[:, part], (0, 0, dz))
-        for d in (1, -1):
-            mine, theirs = (1, 0) if d > 0 else (0, 1)
-            send(px.at[mine, :, part], qx.at[theirs, :, part], (d, 0, dz))
-            send(py.at[mine, :, part], qy.at[theirs, :, part], (0, d, dz))
-            for dy in (1, -1):
-                mine_y, theirs_y = (1, 0) if dy > 0 else (0, 1)
-                send(pc.at[mine, mine_y, part], qc.at[theirs, theirs_y, part], (d, dy, dz))
-    n_z = len(halo)
-    flat = [(0, 1), (0, -1), (1, 0), (-1, 0), (1, 1), (1, -1), (-1, 1), (-1, -1)]
-    for dx, dy in flat:
-        sx4, tx4 = span(dx, W, CX)
-        sy4, ty4 = span(dy, W, CY)
-        sx3, tx3 = span(dx, W - 1, CX)
-        sy3, ty3 = span(dy, W - 1, CY)
-        send(own.at[0:3, sx4, sy4], a.at[:, tx4, ty4], (dx, dy, 0))
-        send(own.at[3:6, sx3, sy3], b.at[:, tx3, ty3], (dx, dy, 0))
-        send(own.at[6, sx3, sy3], c.at[tx3, ty3], (dx, dy, 0))
-
     half = pl.ds(4 * lax.rem(gy, 2), 4)
     spread_y = []
     for k in range(1, N):
@@ -340,8 +377,7 @@
     own_par = pltpu.make_async_copy(ownpar, par.at[gz, gy // 2, :, half], lsem.at[0])
     own_par.start()
 
-    for copy in halo[:n_z]:
-        copy.wait_recv()
+    received(halo[:n_z])
     low_ok = jnp.where(gz > 0, 1, 0)
     high_ok = jnp.where(gz < N - 1, 1, 0)
     keep = jnp.where(lane < CZ // 2, high_ok, low_ok) == 1
@@ -364,11 +400,11 @@
     def store_y(ref, value):
         value = value.reshape(CX, 4, W, CZ)
         ref[W : W + CX, 0:W] = value[:, 0]
-        ref[W : W + CX, W + CY :] = value[:, 1]
+        ref[W : W + CX, W + CY : EY] = value[:, 1]
         ref[0:W, 0:W] = value[:W, 2]
         ref[W + CX :, 0:W] = value[W:, 2]
-        ref[0:W, W + CY :] = value[:W, 3]
-        ref[W + CX :, W + CY :] = value[W:, 3]
+        ref[0:W, W + CY : EY] = value[:W, 3]
+        ref[W + CX :, W + CY : EY] = value[W:, 3]
 
     def unpack_all():
         unpack([qz[f] for f in range(7)], store_own)
@@ -410,8 +446,7 @@
             for xs in parts:
                 clear(xs, slice(W + CY, EY))
 
-    for copy in halo[n_z : n_z + 6]:
-        copy.wait_recv()
+    received(halo[n_z : n_z + 6])
     clear_y([slice(W, W + CX)])
 
     def early():
@@ -437,8 +472,7 @@
         copy.start()
         spread_x.append(copy)
 
-    for copy in halo[n_z + 6 :]:
-        copy.wait_recv()
+    received(halo[n_z + 6 :])
     clear_y([slice(0, W), slice(W + CX, EX)])
 
     @pl.when(gx == 0)
@@ -476,14 +510,15 @@
 
     run("take", take)
     pl.semaphore_wait(plane, N - 1)
-    for k in range(1, N * N):
-        t = lax.rem(me + k, N * N)
+    hops = lambda ky, kz: min(ky, N - ky) + min(kz, N - kz) / 2
+    others = [(ky, kz) for ky in range(N) for kz in range(N) if ky or kz]
+    for ky, kz in sorted(others, key=lambda k: -hops(*k)):
         pltpu.make_async_remote_copy(
             src_ref=ownsam,
             dst_ref=sam.at[gz, gy // 2, half],
             send_sem=ssend,
             recv_sem=srecv,
-            device_id=(gx, lax.rem(t, N), t // N),
+            device_id=near(0, ky, kz),
             device_id_type=MESH,
         ).start()
     own_sam = pltpu.make_async_copy(ownsam, sam.at[gz, gy // 2, half], lsem.at[0])
@@ -531,9 +566,8 @@
 
         def newton(volt, sample, gain, drive, bias, couple, grp, total):
             s = jnp.tanh(volt)
-            shared = jnp.zeros_like(volt)
-            for g in range(GROUPS):
-                shared = jnp.where(grp == float(g + 1), total[g : g + 1], shared)
+            which = jnp.maximum(grp.astype(jnp.int32) - 1, 0)
+            shared = jnp.take_along_axis(total, which, axis=0, mode="promise_in_bounds")
             resid = (1.0 + gain) * volt - sample - bias + drive * s + couple * shared
             slope = 1.0 + gain + (drive + couple) * (1.0 - s * s)
             return volt - resid / slope
@@ -571,16 +605,30 @@
     run("back", back)
     for copy in (out_last, out_next):
         copy.wait()
-    for copy in halo + spread_y + spread_x + twins:
+    for copy, d in halo:
+        if d:
+            pl.when(has(d))(copy.wait_send)
+        else:
+            copy.wait_send()
+    for copy in spread_y + spread_x + twins:
         copy.wait_send()
     pltpu.make_async_copy(drain, drain, ssend).wait()
+
+
+def put_out(e_ref, last_ref, cur_ref, e_out, last_out, cur_out, sem):
+    pairs = ((e_ref, e_out), (last_ref, last_out), (cur_ref, cur_out))
+    copies = [pltpu.make_async_copy(s, d, sem.at[i]) for i, (s, d) in enumerate(pairs)]
+    for copy in copies:
+        copy.start()
+    for copy in copies:
+        copy.wait()
 
 
 def on_device(e, ep, co, cell, route, group, gain, drive, bias, couple):
     line = lambda v: v.reshape(1, PORTS)
     any_spec = pl.BlockSpec(memory_space=pl.ANY)
     dma = pltpu.SemaphoreType.DMA
-    ext, ext1 = pltpu.VMEM((3, EX, EY, CZ), F32), pltpu.VMEM((EX, EY, CZ), F32)
+    ext, ext1 = pltpu.VMEM((3, EX, EY + 8, CZ), F32), pltpu.VMEM((EX, EY + 8, CZ), F32)
     electric, last, current = pl.pallas_call(
         kernel,
         out_shape=(
@@ -621,8 +669,8 @@
             pltpu.VMEM((8, CZ), F32),
             pltpu.VMEM((8, CZ), F32),
             dma((13,)),
-            dma((42,)),
-            dma((42,)),
+            dma((46,)),
+            dma((46,)),
             dma((N - 1,)),
             dma((N - 1,)),
             dma((3,)),
@@ -636,7 +684,18 @@
             collective_id=0, has_side_effects=True, vmem_limit_bytes=56 * 1024 * 1024
         ),
     )(e, ep, co, line(cell), line(route), line(group), line(gain), line(drive), line(bias), line(couple))
-    return electric, last, current.reshape(PORTS)
+    return pl.pallas_call(
+        put_out,
+        out_shape=(
+            jax.ShapeDtypeStruct((3, CX, CY, CZ), F32),
+            jax.ShapeDtypeStruct((3, CX, CY, CZ), F32),
+            jax.ShapeDtypeStruct((PORTS,), F32),
+        ),
+        in_specs=[any_spec] * 3,
+        out_specs=(any_spec,) * 3,
+        scratch_shapes=[dma((3,))],
+        compiler_params=pltpu.CompilerParams(vmem_limit_bytes=1024 * 1024),
+    )(electric, last, current.reshape(PORTS))
 
 
 def solution(mesh):

time: 40.8 us -> 32.8 us (0.80)
  Pallas kernels: 38.1 us -> 31.6 us
  local copies, waits for them, and re-layouts: 1.92 us -> 0 us
    pallas_call x1, Pallas kernels: 38.1 us -> 30.8 us  [on_device(): pl.pallas_call(kernel, out_shape=(pltpu.VMEM((3, CX, CY, CZ), F32), pltpu...]
    unnamed x3 -> x0, local copies, waits for them, and re-layouts: 1.92 us -> none
    pallas_call x0 -> x1, Pallas kernels: none -> 0.77 us  [on_device(): pl.pallas_call(put_out, out_shape=(jax.ShapeDtypeStruct((3, CX, CY, CZ),...]
where the time goes in v3:
time: 32.8 us; the launch traced here: 32.2 us
  Pallas kernels  31.6 us (96%)
  between operations  0.64 us (2%)
    pallas_call x1, Pallas kernels, on_device(): pl.pallas_call(kernel, out_shape=(pltpu.VMEM((3, CX, CY, CZ), F32), pltpu...  30.8 us
    pallas_call x1, Pallas kernels, on_device(): pl.pallas_call(put_out, out_shape=(jax.ShapeDtypeStruct((3, CX, CY, CZ),...  0.77 us

profile of v3, /device:TPU:1, one launch (start us, length us, event | category | flops | bytes accessed | tf_op | source)
XLA Modules:
  0.0 32.2 jit_solution(3594426025591445165)
XLA Ops:
  0.6 30.8 %shard_map.121 = (f32[3,8,16,128]{3,2,1,0:T(8,128)S(1)}, f32[3,8,16,128]{3,2,1,0:T(8,128)S(1)}, f32[1,256]{1,0:T(1,128)S(1)}) custom-call(f32[3,8,16,128]{3,2,1,0:T(8,128)} %e_ref.1, f32[3,8,16,128]{3,2,1,0:T(8,128)} %ep_ref.1, f32[8,16,128]{2,1,0:T(8,128)} %co_ref.1, s32[1,256]{1,0:T(1,128)} %bitcast.9, s32[1,256]{1,0:T(1,128)} %bitcast.10, ...), custom_call_target="tpu_custom_call" | custom-call | tf_op jit(solution)/shard_map/pallas_call | solution.py:632
  31.5 0.8 %shard_map.122 = (f32[3,8,16,128]{3,2,1,0:T(8,128)}, f32[3,8,16,128]{3,2,1,0:T(8,128)}, f32[256]{0:T(256)}) custom-call(f32[3,8,16,128]{3,2,1,0:T(8,128)S(1)} %get-tuple-element.6.e_ref, f32[3,8,16,128]{3,2,1,0:T(8,128)S(1)} %get-tuple-element.7.last_ref, f32[256]{0:T(256)S(1)} %bitcast.8), custom_call_target="tpu_custom_call" | custom-call | tf_op jit(solution)/shard_map/pallas_call | solution.py:687

commit v4 on v3

--- a/solution.py
+++ b/solution.py
@@ -89,8 +89,8 @@
         kz = (gy - gyp) - (gx - down_y(gx))
         old[0, x, 0:EY] = 2.0 * vx - old[0, x, 0:EY] - c * kx
         old[1, x, 0:EY] = 2.0 * vy - old[1, x, 0:EY] - c * ky
-        old[2, x, 0:EY] = 2.0 * vz - old[2, x, 0:EY] - c * kz
         if not last:
+            old[2, x, 0:EY] = 2.0 * vz - old[2, x, 0:EY] - c * kz
             ch = cou_h[x, 0:EY]
             kxh = (gzh - down_y(gzh)) - (gyh - gydh)
             kyh = (gxh - gxdh) - (gzh - gzph)
@@ -103,6 +103,28 @@
     carry = curls(low - 1)
     for x in range(low, high):
         carry = body(x, carry)
+
+
+def last_z(now, now_h, old, cou):
+    lane = lax.broadcasted_iota(jnp.int32, (CY, CZ), 1)
+    mid, below = slice(W, W + CY), slice(W - 1, W + CY - 1)
+
+    def forward(k, x, rows):
+        main, halo = now[k, x, rows], now_h[k, x, rows]
+        ahead = jnp.where(lane == CZ - 1, pltpu.roll(halo, CZ - 1, 1), pltpu.roll(main, CZ - 1, 1))
+        return ahead - main
+
+    def curl_y(x):
+        return forward(0, x, mid) - (now[2, x + 1, mid] - now[2, x, mid])
+
+    gyp = curl_y(W - 1)
+    for x in range(W, W + CX):
+        vz = now[2, x, mid]
+        gx = (now[2, x, W + 1 : W + CY + 1] - vz) - forward(1, x, mid)
+        gxd = (vz - now[2, x, below]) - forward(1, x, below)
+        gy = curl_y(x)
+        old[2, x, mid] = 2.0 * vz - old[2, x, mid] - cou[x, mid] * ((gy - gyp) - (gx - gxd))
+        gyp = gy
 
 
 def kernel(
@@ -494,11 +516,7 @@
     run("late", late)
     out_last = pltpu.make_async_copy(b.at[:, inner[0], inner[1]], last_ref, lsem.at[1])
     out_last.start()
-    run("step4", lambda: substep(b, bh, a, ah, c, ch, 4, EX - 4, True))
-    out_next = pltpu.make_async_copy(
-        a.at[0:2, inner[0], inner[1]], next_ref.at[0:2], lsem.at[2]
-    )
-    out_next.start()
+    run("lastz", lambda: last_z(b, bh, a, c))
 
     def take():
         ez = a[2, W : W + CX, W : W + CY].reshape(CZ, CZ)
@@ -523,6 +541,12 @@
         ).start()
     own_sam = pltpu.make_async_copy(ownsam, sam.at[gz, gy // 2, half], lsem.at[0])
     own_sam.start()
+
+    run("step4", lambda: substep(b, bh, a, ah, c, ch, 4, EX - 4, True))
+    out_next = pltpu.make_async_copy(
+        a.at[0:2, inner[0], inner[1]], next_ref.at[0:2], lsem.at[2]
+    )
+    out_next.start()
 
     for copy in spread_x:
         copy.wait_recv()

time: 32.8 us -> 32.4 us (0.988)
  Pallas kernels: 31.6 us -> 31.2 us
    pallas_call x1, Pallas kernels: 30.8 us -> 30.5 us  [on_device(): pl.pallas_call(kernel, out_shape=(pltpu.VMEM((3, CX, CY, CZ), F32), pltpu...]
where the time goes in v4:
time: 32.4 us; the launch traced here: 31.9 us
  Pallas kernels  31.2 us (96%)
  between operations  0.64 us (2%)
    pallas_call x1, Pallas kernels, on_device(): pl.pallas_call(kernel, out_shape=(pltpu.VMEM((3, CX, CY, CZ), F32), pltpu...  30.5 us
    pallas_call x1, Pallas kernels, on_device(): pl.pallas_call(put_out, out_shape=(jax.ShapeDtypeStruct((3, CX, CY, CZ),...  0.77 us

profile of v4, /device:TPU:1, one launch (start us, length us, event | category | flops | bytes accessed | tf_op | source)
XLA Modules:
  0.0 31.9 jit_solution(13958136181445882534)
XLA Ops:
  0.6 30.5 %shard_map.121 = (f32[3,8,16,128]{3,2,1,0:T(8,128)S(1)}, f32[3,8,16,128]{3,2,1,0:T(8,128)S(1)}, f32[1,256]{1,0:T(1,128)S(1)}) custom-call(f32[3,8,16,128]{3,2,1,0:T(8,128)} %e_ref.1, f32[3,8,16,128]{3,2,1,0:T(8,128)} %ep_ref.1, f32[8,16,128]{2,1,0:T(8,128)} %co_ref.1, s32[1,256]{1,0:T(1,128)} %bitcast.9, s32[1,256]{1,0:T(1,128)} %bitcast.10, ...), custom_call_target="tpu_custom_call" | custom-call | tf_op jit(solution)/shard_map/pallas_call | solution.py:656
  31.1 0.8 %shard_map.122 = (f32[3,8,16,128]{3,2,1,0:T(8,128)}, f32[3,8,16,128]{3,2,1,0:T(8,128)}, f32[256]{0:T(256)}) custom-call(f32[3,8,16,128]{3,2,1,0:T(8,128)S(1)} %get-tuple-element.6.e_ref, f32[3,8,16,128]{3,2,1,0:T(8,128)S(1)} %get-tuple-element.7.last_ref, f32[256]{0:T(256)S(1)} %bitcast.8), custom_call_target="tpu_custom_call" | custom-call | tf_op jit(solution)/shard_map/pallas_call | solution.py:711
